TPU v7x, 32 devices: a whole 2x2x4 slice. The times are simulated.
32 devices in a mesh: gx: 4 (over y, core), gy: 4 (over z), gz: 2 (over x).
Axes of the slice: x: 2, y: 2, z: 4, core: 2. Of those that a mesh axis runs over, the one named last changes fastest.
Arguments:
- positions: float32 [4, 4, 2, 3, 512], P('gx', 'gy', 'gz'), may hold values from 0 to 1
- attributes: bfloat16 [4, 4, 2, 512, 128], P('gx', 'gy', 'gz'), may hold values from -6 to 6
- edge_center: int32 [4, 4, 2, 6144], P('gx', 'gy', 'gz'), may hold values from 0 to 511
- edge_other: int32 [4, 4, 2, 6144], P('gx', 'gy', 'gz'), may hold values from 0 to 2687
- edge_count: int32 [4, 4, 2], P('gx', 'gy', 'gz'), may hold values from 1536 to 6144, as said below
- rim_rows: int32 [4, 4, 2, 8, 128], P('gx', 'gy', 'gz'), may hold values from 0 to 511
- z_rows: int32 [4, 4, 2, 128], P('gx', 'gy', 'gz'), may hold values from 0 to 2559
- w_emb: bfloat16 [128, 256], replicated, may hold values from -0.5 to 0.5
- w_rbf: float32 [8, 256], replicated, may hold values from -2 to 2
- w_chan: bfloat16 [256, 64], replicated, may hold values from -0.375 to 0.375
- w_lat: bfloat16 [256, 256], replicated, may hold values from -0.375 to 0.375
- w_ten: bfloat16 [192, 256], replicated, may hold values from -0.4375 to 0.4375
- w_out: float32 [256], replicated, may hold values from -0.375 to 0.375
Outputs:
- atom_energy: float32 [4, 4, 2, 512], P('gx', 'gy', 'gz')
- forces: float32 [4, 4, 2, 3, 512], P('gx', 'gy', 'gz')
Inputs may be any that keep to these rules, and one draw needn't show every extreme that they name: `edge_count`: a multiple of 128; a device's edge slots below its count are live; some device has 6144.
All inputs are finite; a program needn't handle non-finite values.
Results may differ from a plain program's by a relative error of at most 0.005.
Values may be sent and summed in bfloat16 or wider, within the bound.
No kernel may reach another device: no remote copies, remote signals or barrier semaphores. Data moves between devices by JAX's collectives and lax.ppermute only.
A program may use at most 64 MiB of HBM per device.

v0:
```python
import math

import jax
import jax.numpy as jnp
import numpy as np
from jax import lax
from jax.sharding import PartitionSpec as P

rim_cells = [(0, 0), (0, 1), (0, 2), (1, 0), (1, 2), (2, 0), (2, 1), (2, 2)]
cycle_cells = [
    (cycle_row, cycle_column)
    for cycle_row in range(5)
    for cycle_column in range(5)
    if cycle_row in (0, 4) or cycle_column in (0, 4)
]


def padded(cells, sides, width):
    for axis, dim in sides:
        count = lax.axis_size(axis)
        head = lax.slice_in_dim(cells, 0, width, axis=dim)
        tail = lax.slice_in_dim(cells, cells.shape[dim] - width, cells.shape[dim], axis=dim)
        cells = jnp.concatenate(
            [
                lax.ppermute(tail, axis, [(i, (i + 1) % count) for i in range(count)]),
                cells,
                lax.ppermute(head, axis, [((i + 1) % count, i) for i in range(count)]),
            ],
            axis=dim,
        )
    return cells


def swapped(x, axis, distance):
    return lax.ppermute(x, axis, [(i, i ^ 1 << distance) for i in range(lax.axis_size(axis))])


def source_of(position):
    if position == 0:
        return (-1, 2)
    if position == 4:
        return (1, 0)
    return (0, position - 1)


def shift_table():
    listing = []
    for cycle_row, cycle_column in cycle_cells:
        listing.append([source_of(cycle_row)[0], source_of(cycle_column)[0], 0])
    return np.array(listing, np.float32)


def embed_atoms(atom_rows, w_emb):
    return jax.nn.silu(jnp.dot(atom_rows, w_emb, preferred_element_type=jnp.float32)).astype(
        jnp.bfloat16
    )


def split_parts(values):
    upper = lax.optimization_barrier(values.astype(jnp.bfloat16))
    lower = (values - upper.astype(jnp.float32)).astype(jnp.bfloat16)
    return jnp.stack([upper, lower])


def join_parts(parts):
    return parts[0].astype(jnp.float32) + parts[1].astype(jnp.float32)


def harmonics(directions):
    along_x, along_y, along_z = (directions[0], directions[1], directions[2])
    root_three = 3.0**0.5
    return [
        jnp.ones_like(along_x),
        along_x,
        along_y,
        along_z,
        root_three * along_x * along_y,
        root_three * along_y * along_z,
        root_three * along_z * along_x,
        0.5 * root_three * (along_x * along_x - along_y * along_y),
        0.5 * (3.0 * along_z * along_z - 1.0),
    ]


def latent_of(position_table, feature_table, centers, others, w_rbf):
    separation = position_table[:, others] - position_table[:, centers]
    squared = jnp.sum(separation * separation, axis=0)
    distance = jnp.sqrt(squared + 0.25)
    directions = separation / distance[None, :]
    envelope = 1.0 / (1.0 + squared * squared / 16.0)
    radii = 0.5 + 0.4 * jnp.arange(w_rbf.shape[0]).astype(jnp.float32)
    radial = jnp.exp(-jnp.square((distance[None, :] - radii[:, None]) / 0.5)) * envelope[None, :]
    mixed = lax.dot_general(
        radial,
        w_rbf,
        (((0,), (0,)), ((), ())),
        precision=lax.Precision.HIGHEST,
        preferred_element_type=jnp.float32,
    )
    mixed = (
        mixed
        + feature_table[centers].astype(jnp.float32)
        + feature_table[others].astype(jnp.float32)
    )
    return (jax.nn.silu(mixed).astype(jnp.bfloat16), directions, envelope)


def tensor_terms(latent, directions, centers, live_mask, w_chan, atom_count):
    channel = jnp.dot(latent, w_chan, preferred_element_type=jnp.float32) * live_mask[:, None]
    harmonic = harmonics(directions)
    products = jnp.concatenate([channel * term[:, None] for term in harmonic], axis=1)
    return jax.ops.segment_sum(products, centers, num_segments=atom_count)


def energy_terms(latent, directions, envelope, tensor, centers, live_mask, w_lat, w_ten, w_out):
    harmonic = harmonics(directions)
    gathered = tensor[centers]
    width = gathered.shape[1] // 9
    bands = []
    for lower, upper in ((0, 1), (1, 4), (4, 9)):
        band = gathered[:, lower * width : (lower + 1) * width] * harmonic[lower][:, None]
        for index in range(lower + 1, upper):
            band = (
                band + gathered[:, index * width : (index + 1) * width] * harmonic[index][:, None]
            )
        bands.append(band)
    invariant = jnp.concatenate(bands, axis=1).astype(jnp.bfloat16)
    hidden = jax.nn.silu(
        jnp.dot(latent, w_lat, preferred_element_type=jnp.float32)
        + jnp.dot(invariant, w_ten, preferred_element_type=jnp.float32)
    )
    return jnp.sum(hidden * w_out[None, :], axis=1) * envelope * live_mask


def per_device(
    positions,
    attributes,
    edge_center,
    edge_other,
    edge_count,
    rim_rows,
    z_rows,
    w_emb,
    w_rbf,
    w_chan,
    w_lat,
    w_ten,
    w_out,
):
    cycle_shifts = shift_table()
    own_positions = positions[0, 0, 0]
    own_attr = attributes[0, 0, 0]
    centers = edge_center[0, 0, 0]
    others = edge_other[0, 0, 0]
    live_count = edge_count[0, 0, 0]
    rim_index_rows = rim_rows[0, 0, 0]
    slab_rows = z_rows[0, 0, 0]
    atom_count = own_positions.shape[1]
    rim_len = rim_index_rows.shape[1]
    rim_flat = rim_index_rows.reshape(-1)
    row_width = own_attr.shape[1]
    feat_cells = own_attr[rim_flat].reshape(8, rim_len, row_width)
    place_cells = jnp.transpose(
        split_parts(own_positions[:, rim_flat]).reshape(2, 3, 8, rim_len), (2, 0, 1, 3)
    ).reshape(8, -1, row_width)
    packed = jnp.concatenate([feat_cells, place_cells], axis=1)
    empty_cell = jnp.zeros_like(packed[0])
    rim_grid = jnp.stack(
        [
            packed[0],
            packed[1],
            packed[2],
            packed[3],
            empty_cell,
            packed[4],
            packed[5],
            packed[6],
            packed[7],
        ]
    ).reshape((3, 3) + packed.shape[1:])
    halo_grid = padded(rim_grid, (("gx", 0), ("gy", 1)), 1)
    cycle_stack = jnp.stack(
        [halo_grid[cycle_row, cycle_column] for cycle_row, cycle_column in cycle_cells]
    )
    cycle_rows = cycle_stack[:, :rim_len].reshape(-1, row_width)
    cycle_parts = cycle_stack[:, rim_len:].reshape(16, 2, 3, rim_len)
    cycle_positions = (
        join_parts(jnp.transpose(cycle_parts, (1, 2, 0, 3)))
        + jnp.asarray(cycle_shifts.T)[:, :, None]
    )
    inner_rows = jnp.concatenate([own_attr, cycle_rows], axis=0)
    inner_positions = jnp.concatenate([own_positions, cycle_positions.reshape(3, -1)], axis=1)
    slab_len = slab_rows.shape[0]
    slab_parts = split_parts(inner_positions[:, slab_rows]).reshape(-1, row_width)
    slab_got = swapped(jnp.concatenate([inner_rows[slab_rows], slab_parts], axis=0), "gz", 0)
    slab_positions = join_parts(slab_got[slab_len:].reshape(2, 3, slab_len))
    slab_lift = (1 - 2 * lax.axis_index("gz")).astype(jnp.float32)
    slab_positions = slab_positions + slab_lift * jnp.array([0.0, 0.0, 1.0], jnp.float32)[:, None]
    table_rows = jnp.concatenate([inner_rows, slab_got[:slab_len]], axis=0)
    position_table = jnp.concatenate([inner_positions, slab_positions], axis=1)
    feature_table = embed_atoms(table_rows, w_emb)
    edge_total = centers.shape[0]
    block_rows = math.gcd(1024, edge_total)
    block_count = (live_count + block_rows - 1) // block_rows
    tensor_width = w_chan.shape[1] * 9

    def block_slice(block_index):
        first_edge = block_index * block_rows
        block_centers = lax.dynamic_slice_in_dim(centers, first_edge, block_rows)
        block_others = lax.dynamic_slice_in_dim(others, first_edge, block_rows)
        live_mask = (first_edge + jnp.arange(block_rows) < live_count).astype(jnp.float32)
        return (block_centers, block_others, live_mask)

    def first_part(place_values, block_centers, block_others, live_mask):
        latent, directions, envelope = latent_of(
            place_values, feature_table, block_centers, block_others, w_rbf
        )
        return tensor_terms(latent, directions, block_centers, live_mask, w_chan, atom_count)

    def tensor_step(block_index, running):
        block_centers, block_others, live_mask = block_slice(block_index)
        return running + first_part(position_table, block_centers, block_others, live_mask)

    tensor = 0.125 * lax.fori_loop(
        0, block_count, tensor_step, jnp.zeros((atom_count, tensor_width), jnp.float32)
    )

    def energy_step(block_index, totals):
        atom_values, place_grad, tensor_grad = totals
        block_centers, block_others, live_mask = block_slice(block_index)

        def block_energy(place_values, tensor_values):
            latent, directions, envelope = latent_of(
                place_values, feature_table, block_centers, block_others, w_rbf
            )
            return energy_terms(
                latent,
                directions,
                envelope,
                tensor_values,
                block_centers,
                live_mask,
                w_lat,
                w_ten,
                w_out,
            )

        edge_energy, pullback = jax.vjp(block_energy, position_table, tensor)
        grad_place, grad_tensor = pullback(jnp.ones_like(edge_energy))
        atom_values = atom_values + jax.ops.segment_sum(
            edge_energy, block_centers, num_segments=atom_count
        )
        return (atom_values, place_grad + grad_place, tensor_grad + grad_tensor)

    atom_energy, place_grad, tensor_grad = lax.fori_loop(
        0,
        block_count,
        energy_step,
        (
            jnp.zeros((atom_count,), jnp.float32),
            jnp.zeros_like(position_table),
            jnp.zeros_like(tensor),
        ),
    )

    def chain_step(block_index, place_total):
        block_centers, block_others, live_mask = block_slice(block_index)
        unused, pullback = jax.vjp(
            lambda place_values: first_part(place_values, block_centers, block_others, live_mask),
            position_table,
        )
        return place_total + pullback(0.125 * tensor_grad)[0]

    place_grad = lax.fori_loop(0, block_count, chain_step, place_grad)
    inner_len = atom_count + 16 * rim_len
    slab_back = swapped(place_grad[:, inner_len:], "gz", 0)
    inner_grad = place_grad[:, :inner_len].at[:, slab_rows].add(slab_back)
    own_grad = inner_grad[:, :atom_count]
    cycle_grad = jnp.transpose(inner_grad[:, atom_count:].reshape(3, 16, rim_len), (1, 0, 2))
    halo_back = jnp.zeros((5, 5, 3, rim_len), jnp.float32)
    for cycle_index, (cycle_row, cycle_column) in enumerate(cycle_cells):
        halo_back = halo_back.at[cycle_row, cycle_column].set(cycle_grad[cycle_index])
    rim_back = jnp.zeros((3, 3, 3, rim_len), jnp.float32)
    column_got = padded(jnp.stack([halo_back[:, 0], halo_back[:, 4]]), (("gy", 0),), 1)
    rim_back = rim_back.at[:, 0].add(column_got[0, 1:4]).at[:, 2].add(column_got[3, 1:4])
    halo_back = halo_back.at[0, 1].add(column_got[0, 0]).at[4, 1].add(column_got[0, 4])
    halo_back = halo_back.at[0, 3].add(column_got[3, 0]).at[4, 3].add(column_got[3, 4])
    row_got = padded(jnp.stack([halo_back[0, 1:4], halo_back[4, 1:4]]), (("gx", 0),), 1)
    rim_back = rim_back.at[0].add(row_got[0]).at[2].add(row_got[3])
    rim_stack = jnp.stack([rim_back[cell_row, cell_column] for cell_row, cell_column in rim_cells])
    own_grad = own_grad.at[:, rim_flat].add(jnp.transpose(rim_stack, (1, 0, 2)).reshape(3, -1))
    return (atom_energy[None, None, None], (-own_grad)[None, None, None])


def solution(mesh):
    return jax.shard_map(
        per_device,
        mesh=mesh,
        in_specs=(
            P("gx", "gy", "gz", None, None),
            P("gx", "gy", "gz", None, None),
            P("gx", "gy", "gz", None),
            P("gx", "gy", "gz", None),
            P("gx", "gy", "gz"),
            P("gx", "gy", "gz", None, None),
            P("gx", "gy", "gz", None),
            P(),
            P(),
            P(),
            P(),
            P(),
            P(),
        ),
        out_specs=(P("gx", "gy", "gz", None), P("gx", "gy", "gz", None, None)),
        check_vma=False,
    )
```

profile of v0, /device:TPU:0, one launch (start us, length us, event | category | flops | bytes accessed | tf_op | source)
XLA Modules:
  0.0 1279.1 jit_solution(9156217994197774286)
XLA Ops:
  39.0 129.7 %while.64 = (s32[]{:T(128)}, f32[512,576]{1,0:T(8,128)S(1)}, s32[]{:T(128)}, s32[6144]{0:T(1024)S(1)}, s32[6144]{0:T(1024)S(1)}, /*index=5*/f32[3,2688]{0,1:T(8,...) while((s32[]{:T(128)}, f32[512,576]{1,0:T(8,128)S(1)}, ...), condition=%wide.region_3.4_spmd, body=%wide.region_0.3_spmd.sunk | while | flops 62342172 | bytes 21029128 | solution.py:224
  73.9 8.4 scatter_fusion
  117.1 8.4 scatter_fusion
  160.4 8.4 scatter_fusion
  171.3 307.9 %while.65 = (s32[]{:T(128)}, f32[512]{0:T(512)S(1)}, f32[3,2688]{0,1:T(8,128)}, f32[512,576]{1,0:T(8,128)S(1)}, s32[]{:T(128)}, /*index=5*/s32[6144]{0:T(1024)S(...) while((s32[]{:T(128)}, f32[512]{0:T(512)S(1)}, ...), condition=%wide.region_21.22_spmd, body=%wide.region_4.21_spmd.sunk | while | flops 542212096 | bytes 69607752 | solution.py:255
  183.3 6.8 gather_fusion.6
  234.0 7.6 scatter_fusion.1
  244.3 13.1 %scatter_fusion.2 = f32[3,2688]{0,1:T(8,128)} fusion(f32[3,2688]{0,1:T(8,128)} %get-tuple-element.1612, s32[2048]{0:T(1024)} %bitcast.399, f32[2048,3]{1,0:T(8,128)} %copy.376), kind=kCustom, calls=%fused_computation.20.clone.1 | custom fusion | flops 6144 | bytes 81920 | tf_op jit(solution)/shard_map/while/body/transpose(jvp())/add_any | solution.py:86
  262.5 8.4 scatter_fusion.3
  282.7 6.8 gather_fusion.6
  333.3 7.6 scatter_fusion.1
  343.7 13.1 %scatter_fusion.2 = f32[3,2688]{0,1:T(8,128)} fusion(f32[3,2688]{0,1:T(8,128)} %get-tuple-element.1612, s32[2048]{0:T(1024)} %bitcast.399, f32[2048,3]{1,0:T(8,128)} %copy.376), kind=kCustom, calls=%fused_computation.20.clone.1 | custom fusion | flops 6144 | bytes 81920 | tf_op jit(solution)/shard_map/while/body/transpose(jvp())/add_any | solution.py:86
  361.9 8.4 scatter_fusion.3
  382.1 6.8 gather_fusion.6
  432.7 7.6 scatter_fusion.1
  443.0 13.1 %scatter_fusion.2 = f32[3,2688]{0,1:T(8,128)} fusion(f32[3,2688]{0,1:T(8,128)} %get-tuple-element.1612, s32[2048]{0:T(1024)} %bitcast.399, f32[2048,3]{1,0:T(8,128)} %copy.376), kind=kCustom, calls=%fused_computation.20.clone.1 | custom fusion | flops 6144 | bytes 81920 | tf_op jit(solution)/shard_map/while/body/transpose(jvp())/add_any | solution.py:86
  461.2 8.4 scatter_fusion.3
  479.7 166.2 %while.66 = (s32[]{:T(128)}, f32[3,2688]{0,1:T(8,128)}, s32[]{:T(128)}, s32[6144]{0:T(1024)S(1)}, s32[6144]{0:T(1024)S(1)}, /*index=5*/f32[3,2688]{0,1:T(8,128)}...) while((s32[]{:T(128)}, f32[3,2688]{0,1:T(8,128)}, ...), condition=%wide.region_36.37_spmd, body=%wide.region_22.36_spmd.sunk | while | flops 126082080 | bytes 29493640 | solution.py:274
  489.7 6.8 gather_fusion.11
  522.0 13.1 %scatter_fusion.4 = f32[3,2688]{0,1:T(8,128)} fusion(f32[3,2688]{0,1:T(8,128)} %get-tuple-element.1664, s32[2048]{0:T(1024)S(1)} %bitcast.398, f32[2048,3]{1,0:T(8,128)} %copy.381), kind=kCustom, calls=%fused_computation.22.clone.1 | custom fusion | flops 6144 | bytes 81920 | tf_op jit(solution)/shard_map/while/body/transpose(jvp())/add_any | solution.py:86
  577.4 13.1 %scatter_fusion.4 = f32[3,2688]{0,1:T(8,128)} fusion(f32[3,2688]{0,1:T(8,128)} %get-tuple-element.1664, s32[2048]{0:T(1024)S(1)} %bitcast.398, f32[2048,3]{1,0:T(8,128)} %copy.381), kind=kCustom, calls=%fused_computation.22.clone.1 | custom fusion | flops 6144 | bytes 81920 | tf_op jit(solution)/shard_map/while/body/transpose(jvp())/add_any | solution.py:86
  632.8 13.1 %scatter_fusion.4 = f32[3,2688]{0,1:T(8,128)} fusion(f32[3,2688]{0,1:T(8,128)} %get-tuple-element.1664, s32[2048]{0:T(1024)S(1)} %bitcast.398, f32[2048,3]{1,0:T(8,128)} %copy.381), kind=kCustom, calls=%fused_computation.22.clone.1 | custom fusion | flops 6144 | bytes 81920 | tf_op jit(solution)/shard_map/while/body/transpose(jvp())/add_any | solution.py:86
  664.8 396.7 %collective-permute-start.6 = (f32[1,5,3,128]{3,1,2,0:T(8,128)S(1)}, f32[1,5,3,128]{3,1,2,0:T(8,128)S(1)}, u32[]{:S(2)}, u32[]{:S(2)}) collective-permute-start(f32[1,5,3,128]{3,1,2,0:T(8,128)S(1)} %copy.327), channel_id=1, source_target_pairs={{0,2},{2,4},{4,6},{6,0},{1,3},{3,5},{5,7},{7,1},{8,10},{10,12},{12... | collective-permute-start | bytes 23048 | tf_op jit(solution)/shard_map/ppermute | solution.py:25
  1069.1 199.6 %collective-permute-start.9 = (f32[1,3,3,128]{3,0,2,1:T(1,128)S(1)}, f32[1,3,3,128]{3,0,2,1:T(1,128)S(1)}, u32[]{:S(2)}, u32[]{:S(2)}) collective-permute-start(f32[1,3,3,128]{3,0,2,1:T(1,128)S(1)} %get-tuple-element.1071), channel_id=1, source_target_pairs={{8,0},{16,8},{24,16},{0,24},{9,1},{17,9},{25,17},{1,25},{10,2},{18... | collective-permute-start | bytes 13832 | tf_op jit(solution)/shard_map/ppermute | solution.py:27
  (671 shorter events, 489.4 us)
Async XLA Ops:
  0.6 37.3 %copy-start = (bf16[128,256]{1,0:T(8,128)(2,1)S(1)}, bf16[128,256]{1,0:T(8,128)(2,1)}, u32[]{:S(2)}) copy-start(bf16[128,256]{1,0:T(8,128)(2,1)} %param.76) | copy-start | bytes 196612
  10.0 5.7 collective-permute-start.1
  12.5 4.3 collective-permute-start
  13.2 15.0 %copy-start.41 = (f32[3,16]{0,1:T(8,128)S(1)}, f32[3,16]{0,1:T(8,128)}, u32[]{:S(2)}) copy-start(f32[3,16]{0,1:T(8,128)} %constant.1010.clone) | copy-start | bytes 580
  16.8 9.2 collective-permute-start.2
  18.5 9.0 collective-permute-start.3
  32.3 4.0 collective-permute-start.4
  171.6 11.8 copy-start.20
  241.6 15.8 %copy-start.12 = (f32[1024,192]{0,1:T(8,128)S(1)}, f32[1024,192]{0,1:T(8,128)}, u32[]{:S(2)}) copy-start(f32[1024,192]{0,1:T(8,128)} %copy-done.11) | copy-start | bytes 2359300 | tf_op jit(solution)/shard_map/while
  341.0 15.8 %copy-start.12 = (f32[1024,192]{0,1:T(8,128)S(1)}, f32[1024,192]{0,1:T(8,128)}, u32[]{:S(2)}) copy-start(f32[1024,192]{0,1:T(8,128)} %copy-done.11) | copy-start | bytes 2359300 | tf_op jit(solution)/shard_map/while
  440.3 15.8 %copy-start.12 = (f32[1024,192]{0,1:T(8,128)S(1)}, f32[1024,192]{0,1:T(8,128)}, u32[]{:S(2)}) copy-start(f32[1024,192]{0,1:T(8,128)} %copy-done.11) | copy-start | bytes 2359300 | tf_op jit(solution)/shard_map/while
  479.7 20.0 %copy-start.32 = (s32[6144]{0:T(1024)}, s32[6144]{0:T(1024)S(1)}, u32[]{:S(2)}) copy-start(s32[6144]{0:T(1024)S(1)} %get-tuple-element.1681) | copy-start | bytes 73732 | tf_op jit(solution)/shard_map/while
  519.1 16.0 %copy-start.33 = (s32[6144]{0:T(1024)S(1)}, s32[6144]{0:T(1024)}, u32[]{:S(2)}) copy-start(s32[6144]{0:T(1024)} %copy-done.32) | copy-start | bytes 73732 | tf_op jit(solution)/shard_map/while
  535.1 19.9 %copy-start.32 = (s32[6144]{0:T(1024)}, s32[6144]{0:T(1024)S(1)}, u32[]{:S(2)}) copy-start(s32[6144]{0:T(1024)S(1)} %get-tuple-element.1681) | copy-start | bytes 73732 | tf_op jit(solution)/shard_map/while
  574.5 16.0 %copy-start.33 = (s32[6144]{0:T(1024)S(1)}, s32[6144]{0:T(1024)}, u32[]{:S(2)}) copy-start(s32[6144]{0:T(1024)} %copy-done.32) | copy-start | bytes 73732 | tf_op jit(solution)/shard_map/while
  590.5 19.9 %copy-start.32 = (s32[6144]{0:T(1024)}, s32[6144]{0:T(1024)S(1)}, u32[]{:S(2)}) copy-start(s32[6144]{0:T(1024)S(1)} %get-tuple-element.1681) | copy-start | bytes 73732 | tf_op jit(solution)/shard_map/while
  629.9 16.0 %copy-start.33 = (s32[6144]{0:T(1024)S(1)}, s32[6144]{0:T(1024)}, u32[]{:S(2)}) copy-start(s32[6144]{0:T(1024)} %copy-done.32) | copy-start | bytes 73732 | tf_op jit(solution)/shard_map/while
  646.8 4.3 collective-permute-start.5
  652.9 619.1 %copy-start.39 = (s32[1024,1]{0,1:T(1,128)S(1)}, s32[1024,1]{0,1:T(1,128)}, u32[]{:S(2)}) copy-start(s32[1024,1]{0,1:T(1,128)} %copy-done.38) | copy-start | bytes 12292
  652.9 626.0 %copy-start.1 = (bf16[128,256]{1,0:T(8,128)(2,1)S(1)}, bf16[128,256]{1,0:T(8,128)(2,1)}, u32[]{:S(2)}) copy-start(bf16[128,256]{1,0:T(8,128)(2,1)} %param.76) | copy-start | bytes 196612
  664.8 398.1 %collective-permute-start.6 = (f32[1,5,3,128]{3,1,2,0:T(8,128)S(1)}, f32[1,5,3,128]{3,1,2,0:T(8,128)S(1)}, u32[]{:S(2)}, u32[]{:S(2)}) collective-permute-start(f32[1,5,3,128]{3,1,2,0:T(8,128)S(1)} %copy.327), channel_id=1, source_target_pairs={{0,2},{2,4},{4,6},{6,0},{1,3},{3,5},{5,7},{7,1},{8,10},{10,12},{12... | collective-permute-start | bytes 23048 | tf_op jit(solution)/shard_map/ppermute | solution.py:25
  1061.6 4.1 collective-permute-start.7
  1069.1 200.9 %collective-permute-start.9 = (f32[1,3,3,128]{3,0,2,1:T(1,128)S(1)}, f32[1,3,3,128]{3,0,2,1:T(1,128)S(1)}, u32[]{:S(2)}, u32[]{:S(2)}) collective-permute-start(f32[1,3,3,128]{3,0,2,1:T(1,128)S(1)} %get-tuple-element.1071), channel_id=1, source_target_pairs={{8,0},{16,8},{24,16},{0,24},{9,1},{17,9},{25,17},{1,25},{10,2},{18... | collective-permute-start | bytes 13832 | tf_op jit(solution)/shard_map/ppermute | solution.py:27
  1268.7 3.0 collective-permute-start.8
  (102 other events, 473.5 us)
where the time goes:
time: 1300 us; the launch traced here: 1280 us
  starting transfers between devices  606 us (47%)
  local copies, waits for them, and re-layouts  336 us (26%)
  other arithmetic  244 us (19%)
  matrix products  64.8 us (5%)
  waiting for transfers between devices  14.5 us (1%)
    ppermute x4, starting transfers between devices, padded(): lax.ppermute(tail, axis, [(i, (i + 1) % count) for i in range(count)])  398 us
    ppermute x4, starting transfers between devices, padded(): lax.ppermute(head, axis, [((i + 1) % count, i) for i in range(count)])  204 us
    gather x30, local copies, waits for them, and re-layouts, latent_of(): separation = position_table[:, others] - position_table[:, centers]  80.4 us
    add_any x6, other arithmetic, latent_of(): separation = position_table[:, others] - position_table[:, centers]  78.6 us
    gather x9, local copies, waits for them, and re-layouts, latent_of(): feature_table[centers].astype(jnp.float32)  45.5 us
    gather x9, local copies, waits for them, and re-layouts, latent_of(): feature_table[others].astype(jnp.float32)  41.4 us
    while x231, local copies, waits for them, and re-layouts  39.4 us
    dot_general x15, matrix products, latent_of(): lax.dot_general(radial, w_rbf, (((0,), (0,)), ((), ())), precision=lax.Pr...  31.7 us
  transfers between devices with their start and end apart: 10, of which 9 were waited for; matrix products, arithmetic and copies ran while one was open for 1% of the time, Pallas kernels for 0%

commit v1 on v0

v1 whole, which is shorter than its diff:
```python
import jax
import jax.numpy as jnp
from jax import lax
from jax.experimental import pallas as pl
from jax.experimental.pallas import tpu as pltpu
from jax.sharding import PartitionSpec as P

f32 = jnp.float32
bf16 = jnp.bfloat16
LANES = 128
PARTS = 16
ROOT3 = 3.0**0.5
BANDS = (0, 1, 1, 1, 2, 2, 2, 2, 2)

rim_cells = [(0, 0), (0, 1), (0, 2), (1, 0), (1, 2), (2, 0), (2, 1), (2, 2)]
cycle_cells = [(p, q) for p in range(5) for q in range(5) if p in (0, 4) or q in (0, 4)]


def source_of(position):
    if position == 0:
        return (-1, 2)
    if position == 4:
        return (1, 0)
    return (0, position - 1)


routes = {}
for _cycle, (_p, _q) in enumerate(cycle_cells):
    (_sx, _a), (_sy, _b) = source_of(_p), source_of(_q)
    routes.setdefault((_sx, _sy), []).append((_cycle, rim_cells.index((_a, _b))))
directions = sorted(routes, key=lambda way: (-len(routes[way]), way))


def dot(a, b):
    return lax.dot_general(a, b, (((1,), (0,)), ((), ())), preferred_element_type=f32)


def dot_t(a, b):
    return lax.dot_general(a, b, (((1,), (1,)), ((), ())), preferred_element_type=f32)


def rows_of(shape):
    return lax.broadcasted_iota(jnp.int32, shape, 0)


def one_hot(index, size):
    return jnp.where(rows_of((size, index.shape[1])) == index, 1.0, 0.0)


def halves(values):
    upper = values.astype(bf16).astype(f32)
    return upper, values - upper


def masked(hot_low, high16, value):
    mask = jnp.where(high16 == value, 1.0, 0.0).astype(bf16)
    size, lanes = hot_low.shape
    return (hot_low.reshape(size // 16, 16, lanes) * mask[None]).reshape(size, lanes)


def sigmoid(x):
    return 0.5 * jnp.tanh(0.5 * x) + 0.5


def pack_kernel(pos_ref, attr_ref, rim_ref, own_ref, *rest):
    sends, parts = rest[:-1], rest[-1]
    atoms, width = attr_ref.shape
    eye = jnp.where(
        rows_of((width, width)) == lax.broadcasted_iota(jnp.int32, (width, width), 1), 1.0, 0.0
    ).astype(bf16)
    own_ref[0:width, :] = dot_t(eye, attr_ref[...]).astype(bf16)
    upper, lower = halves(pos_ref[...])
    parts[...] = jnp.zeros_like(parts)
    parts[0:3, :] = upper
    parts[3:6, :] = lower
    own_ref[width : width + PARTS, :] = parts[...].astype(bf16)
    packed = own_ref[...]
    for rim in range(8):
        hot = one_hot(rim_ref[rim : rim + 1, :], atoms).astype(bf16)
        cell = dot(packed, hot).astype(bf16)
        for way, send in zip(directions, sends):
            for slot, (_, source) in enumerate(routes[way]):
                if source == rim:
                    send[:, slot * LANES : (slot + 1) * LANES] = cell


def slab_kernel(pos_ref, own_ref, zrows_ref, *rest):
    got, (inner_ref, send_ref, parts) = rest[:8], rest[8:]
    atoms = own_ref.shape[1]
    height = own_ref.shape[0]
    width = height - PARTS
    inner_len = inner_ref.shape[1]
    inner_ref[:, 0:atoms] = own_ref[...]
    parts[...] = jnp.zeros_like(parts)
    upper, lower = halves(pos_ref[...])
    parts[0:3, 0:atoms] = upper
    parts[3:6, 0:atoms] = lower
    for way, ref in zip(directions, got):
        for slot, (cycle, _) in enumerate(routes[way]):
            lanes = slice(slot * LANES, (slot + 1) * LANES)
            into = slice(atoms + cycle * LANES, atoms + (cycle + 1) * LANES)
            inner_ref[0:width, into] = ref[0:width, lanes]
            arrived = ref[width:height, lanes].astype(f32)
            joined = arrived[0:3] + arrived[3:6]
            axis = rows_of((3, LANES))
            shift = jnp.where(axis == 0, float(way[0]), jnp.where(axis == 1, float(way[1]), 0.0))
            upper, lower = halves(joined + shift)
            parts[0:3, into] = upper
            parts[3:6, into] = lower
    inner_ref[width:height, :] = parts[...].astype(bf16)
    hot = one_hot(zrows_ref[...], inner_len).astype(bf16)
    send_ref[...] = dot(inner_ref[...], hot).astype(bf16)


def embed_kernel(inner_ref, w_emb_ref, feat_ref, place_ref):
    width = w_emb_ref.shape[1]
    inner_len = inner_ref.shape[1]
    for first in range(0, inner_len, 512):
        raw = dot(w_emb_ref[...], inner_ref[0:width, first : first + 512])
        feat_ref[:, first : first + 512] = (raw * sigmoid(raw)).astype(bf16)
    parts = inner_ref[width:, :].astype(f32)
    place_ref[...] = jnp.zeros_like(place_ref)
    for high in range(inner_len // LANES):
        place_ref[0:6, high, :] = parts[0:6, high * LANES : (high + 1) * LANES]


def harmonic_rows(x, y, z):
    return [
        None,
        x,
        y,
        z,
        ROOT3 * x * y,
        ROOT3 * y * z,
        ROOT3 * z * x,
        0.5 * ROOT3 * (x * x - y * y),
        0.5 * (3.0 * z * z - 1.0),
    ]


def fold8(values):
    return jnp.sum(values.reshape(values.shape[0] // 8, 8, values.shape[1]), axis=0)


def edge_kernel(
    count_ref,
    lift_ref,
    centers_ref,
    others_ref,
    feat_in_ref,
    place_in_ref,
    slab_ref,
    w_emb_ref,
    w_rad_ref,
    w_chan_t_ref,
    w_chan_ref,
    w_lat_t_ref,
    w_ten_t_ref,
    w_back_ref,
    w_out_ref,
    w_rbf_ref,
    grad_ref,
    energy_ref,
    feat,
    place,
    hot,
    center_hot,
    low_o,
    low_c,
    latent_s,
    slope_s,
    chan_s,
    geo_s,
    dlat_s,
    dharm_s,
    tensor,
    tensor_b,
    dtensor,
    acc_o,
    acc_c,
):
    blocks, _, eb = centers_ref.shape
    width = w_emb_ref.shape[1]
    features = feat_in_ref.shape[0]
    inner_len = feat_in_ref.shape[1]
    table = inner_len + LANES
    highs = table // LANES
    atoms = tensor.shape[1]
    c_highs = atoms // LANES
    chans = w_chan_t_ref.shape[0]
    hpad = place_in_ref.shape[1]
    count = count_ref[0]

    feat[:, 0:inner_len] = feat_in_ref[...]
    raw = dot(w_emb_ref[...], slab_ref[0:width, :])
    feat[:, inner_len:table] = (raw * sigmoid(raw)).astype(bf16)
    feat[:, table : table + LANES] = w_rad_ref[...]
    place[...] = place_in_ref[...]
    arrived = slab_ref[width:, :].astype(f32)
    joined = arrived[0:3] + arrived[3:6]
    joined = joined + jnp.where(rows_of((3, LANES)) == 2, lift_ref[0], 0.0)
    upper, lower = halves(joined)
    place[0:3, highs - 1, :] = upper
    place[3:6, highs - 1, :] = lower
    hot[table:, :] = jnp.zeros((hot.shape[0] - table, eb), bf16)
    tensor[...] = jnp.zeros_like(tensor)
    dtensor[...] = jnp.zeros_like(dtensor)
    acc_o[...] = jnp.zeros_like(acc_o)
    acc_c[...] = jnp.zeros_like(acc_c)

    def first_pass(b, carry):
        c = centers_ref[b]
        o = others_ref[b]
        live = jnp.where(
            lax.broadcasted_iota(jnp.int32, (1, eb), 1) + b * eb < count, 1.0, 0.0
        )
        c_high = lax.shift_right_logical(c, 7)
        o_high = lax.shift_right_logical(o, 7)
        hot_c = one_hot(lax.bitwise_and(c, LANES - 1), LANES).astype(bf16)
        hot_o = one_hot(lax.bitwise_and(o, LANES - 1), LANES).astype(bf16)
        low_c[b] = hot_c
        low_o[b] = hot_o
        c_high16 = jnp.broadcast_to(c_high, (16, eb))
        o_high16 = jnp.broadcast_to(o_high, (16, eb))

        place_rows = place[...].reshape(6 * hpad, LANES).astype(bf16)
        picked = dot(place_rows, hot_o)
        picked = (picked[0 : 3 * hpad] + picked[3 * hpad :]).reshape(3, hpad, eb)
        po = jnp.sum(picked * one_hot(o_high, hpad)[None], axis=1)
        own_rows = place[:, 0:8, :].reshape(48, LANES).astype(bf16)
        picked = dot(own_rows, hot_c)
        picked = (picked[0:24] + picked[24:48]).reshape(3, 8, eb)
        pc = jnp.sum(picked * one_hot(c_high, 8)[None], axis=1)
        sep = po - pc
        rx, ry, rz = sep[0:1], sep[1:2], sep[2:3]
        squared = rx * rx + ry * ry + rz * rz
        inv_d = lax.rsqrt(squared + 0.25)
        dist = (squared + 0.25) * inv_d
        env = 1.0 / (1.0 + squared * squared * (1.0 / 16.0))
        x, y, z = rx * inv_d, ry * inv_d, rz * inv_d
        for row, value in enumerate((x, y, z, inv_d, dist, env, squared, live)):
            geo_s[b, row : row + 1, :] = value
        mu = 0.5 + 0.4 * rows_of((8, eb)).astype(f32)
        u = (dist - mu) * 2.0
        upper, lower = halves(jnp.exp(-(u * u)) * env)
        radial = jnp.concatenate([upper, lower], axis=0).astype(bf16)
        hot[table : table + 16, :] = radial
        hot[table + 16 : table + 32, :] = radial

        for high in range(highs):
            chunk = masked(hot_o, o_high16, high)
            if high < c_highs:
                own = masked(hot_c, c_high16, high)
                center_hot[b, high * LANES : (high + 1) * LANES, :] = own
                chunk = chunk + own
            hot[high * LANES : (high + 1) * LANES, :] = chunk

        mixed = dot(feat[...], hot[...])
        s = sigmoid(mixed)
        value = mixed * s
        latent = value.astype(bf16)
        latent_s[b] = latent
        slope_s[b] = (s + value * (1.0 - s)).astype(bf16)
        chan = dot(w_chan_t_ref[...], latent) * live
        chan_s[b] = chan
        harm = harmonic_rows(x, y, z)
        products = jnp.concatenate(
            [(chan if h is None else chan * h).astype(bf16) for h in harm], axis=0
        )
        tensor[...] += dot_t(products, center_hot[b])
        return carry

    lax.fori_loop(0, blocks, first_pass, 0)
    tensor_b[...] = (0.125 * tensor[...]).astype(bf16)

    def second_pass(b, carry):
        geo = geo_s[b]
        x, y, z = geo[0:1], geo[1:2], geo[2:3]
        env, live = geo[5:6], geo[7:8]
        harm = harmonic_rows(x, y, z)
        gathered = dot(tensor_b[...], center_hot[b])
        parts = [gathered[m * chans : (m + 1) * chans] for m in range(9)]
        bands = [parts[0], None, None]
        for m in range(1, 9):
            term = parts[m] * harm[m]
            band = BANDS[m]
            bands[band] = term if bands[band] is None else bands[band] + term
        invariant = jnp.concatenate([band.astype(bf16) for band in bands], axis=0)
        pre = dot(w_lat_t_ref[...], latent_s[b]) + dot(w_ten_t_ref[...], invariant)
        s = sigmoid(pre)
        value = pre * s
        weight = w_out_ref[...]
        summed = jnp.sum(value * weight, axis=0, keepdims=True)
        geo_s[b, 8:9, :] = summed
        dpre = (weight * (env * live) * (s + value * (1.0 - s))).astype(bf16)
        back = dot(w_back_ref[...], dpre)
        dlat_s[b] = back[0:features].astype(bf16)
        dbands = [
            back[features + band * chans : features + (band + 1) * chans] for band in range(3)
        ]
        products = jnp.concatenate(
            [
                (dbands[BANDS[m]] if harm[m] is None else dbands[BANDS[m]] * harm[m]).astype(bf16)
                for m in range(9)
            ],
            axis=0,
        )
        dtensor[...] += dot_t(products, center_hot[b])
        for m in range(1, 9):
            dharm_s[b, (m - 1) * 8 : m * 8, :] = fold8(dbands[BANDS[m]] * parts[m])
        return carry

    lax.fori_loop(0, blocks, second_pass, 0)
    tensor_b[...] = (0.125 * dtensor[...]).astype(bf16)

    def third_pass(b, carry):
        geo = geo_s[b]
        x, y, z = geo[0:1], geo[1:2], geo[2:3]
        inv_d, dist, env, squared = geo[3:4], geo[4:5], geo[5:6], geo[6:7]
        live, summed = geo[7:8], geo[8:9]
        harm = harmonic_rows(x, y, z)
        gathered = dot(tensor_b[...], center_hot[b])
        chan = chan_s[b]
        dchan = gathered[0:chans]
        dh = [None]
        for m in range(1, 9):
            part = gathered[m * chans : (m + 1) * chans]
            dchan = dchan + part * harm[m]
            total = dharm_s[b, (m - 1) * 8 : m * 8, :] + fold8(part * chan)
            dh.append(jnp.sum(total, axis=0, keepdims=True))
        dchan = (dchan * live).astype(bf16)
        dlat = dlat_s[b].astype(f32) + dot(w_chan_ref[...], dchan)
        dmixed = (dlat * slope_s[b].astype(f32)).astype(bf16)
        drad = dot(w_rbf_ref[...], dmixed)
        drad = drad[0:8] + drad[8:16]
        mu = 0.5 + 0.4 * rows_of((8, eb)).astype(f32)
        u = (dist - mu) * 2.0
        weighted = drad * jnp.exp(-(u * u))
        denv = jnp.sum(weighted, axis=0, keepdims=True) + live * summed
        ddist = -4.0 * env * jnp.sum(weighted * u, axis=0, keepdims=True)
        dx = dh[1] + ROOT3 * (y * dh[4] + z * dh[6] + x * dh[7])
        dy = dh[2] + ROOT3 * (x * dh[4] + z * dh[5] - y * dh[7])
        dz = dh[3] + ROOT3 * (y * dh[5] + x * dh[6]) + 3.0 * z * dh[8]
        ddist = ddist - (dx * x + dy * y + dz * z) * inv_d
        dsq = denv * (env * env * squared * -0.125) + ddist * (0.5 * inv_d)
        both = 2.0 * dsq * dist
        gs = [dx * inv_d + both * x, dy * inv_d + both * y, dz * inv_d + both * z]
        energy = summed * env * live

        c_high = lax.shift_right_logical(centers_ref[b], 7)
        o_high = lax.shift_right_logical(others_ref[b], 7)
        mask_o = one_hot(o_high, hpad)
        mask_c = one_hot(c_high, 8)
        split = [halves(g) for g in gs]
        rows_o = jnp.concatenate(
            [mask_o * split[d][part] for part in range(2) for d in range(3)], axis=0
        ).astype(bf16)
        split.append(halves(energy))
        rows_c = jnp.concatenate(
            [mask_c * split[d][part] for part in range(2) for d in range(4)], axis=0
        ).astype(bf16)
        acc_o[...] += dot_t(rows_o, low_o[b])
        acc_c[...] += dot_t(rows_c, low_c[b])
        return carry

    lax.fori_loop(0, blocks, third_pass, 0)
    sum_o = acc_o[0 : 3 * hpad, :] + acc_o[3 * hpad :, :]
    sum_c = acc_c[0:32, :] + acc_c[32:64, :]
    for d in range(3):
        grad_ref[d] = sum_o[d * hpad : (d + 1) * hpad]
        grad_ref[d, 0:8, :] = sum_o[d * hpad : d * hpad + 8] - sum_c[d * 8 : (d + 1) * 8]
    energy_ref[...] = sum_c[24:32]


def return_kernel(grad_ref, back_ref, zrows_ref, own_ref, *sends):
    hpad = grad_ref.shape[1]
    z_rows = zrows_ref[...]
    mask = one_hot(lax.shift_right_logical(z_rows, 7), hpad)
    low = one_hot(lax.bitwise_and(z_rows, LANES - 1), LANES).astype(bf16)
    pieces = [halves(back_ref[d : d + 1, :]) for d in range(3)]
    rows = jnp.concatenate(
        [mask * pieces[d][part] for part in range(2) for d in range(3)], axis=0
    ).astype(bf16)
    landed = dot_t(rows, low)
    landed = landed[0 : 3 * hpad] + landed[3 * hpad :]
    base = own_ref.shape[1] // 2
    for d in range(3):
        total = grad_ref[d] + landed[d * hpad : (d + 1) * hpad]
        own_ref[d] = total[0:8]
        for way, send in zip(directions, sends):
            for slot, (cycle, _) in enumerate(routes[way]):
                row = base + cycle
                send[slot * 3 + d : slot * 3 + d + 1, :] = total[row : row + 1]


def force_kernel(own_ref, rim_ref, *rest):
    got, (out_ref, rim_sum) = rest[:8], rest[8:]
    rim_sum[...] = jnp.zeros_like(rim_sum)
    for way, ref in zip(directions, got):
        for slot, (_, rim) in enumerate(routes[way]):
            rim_sum[rim, 0:3, :] += ref[slot * 3 : slot * 3 + 3, :]
    total = jnp.zeros((48, LANES), f32)
    for rim in range(8):
        index = rim_ref[rim : rim + 1, :]
        mask = one_hot(lax.shift_right_logical(index, 7), 8)
        low = one_hot(lax.bitwise_and(index, LANES - 1), LANES).astype(bf16)
        values = rim_sum[rim]
        pieces = [halves(values[d : d + 1, :]) for d in range(3)]
        rows = jnp.concatenate(
            [mask * pieces[d][part] for part in range(2) for d in range(3)], axis=0
        ).astype(bf16)
        total = total + dot_t(rows, low)
    total = total[0:24] + total[24:48]
    for d in range(3):
        for high in range(out_ref.shape[1] // LANES):
            value = own_ref[d, high : high + 1, :] + total[d * 8 + high : d * 8 + high + 1, :]
            out_ref[d : d + 1, high * LANES : (high + 1) * LANES] = -value


def call(kernel, out_shape, args, scratch=(), smem=0, limit=None):
    vmem = pl.BlockSpec(memory_space=pltpu.VMEM)
    scalar = pl.BlockSpec(memory_space=pltpu.SMEM)
    return pl.pallas_call(
        kernel,
        out_shape=out_shape,
        in_specs=[scalar] * smem + [vmem] * (len(args) - smem),
        out_specs=jax.tree.map(lambda _: vmem, out_shape),
        scratch_shapes=list(scratch),
        compiler_params=pltpu.CompilerParams(vmem_limit_bytes=limit),
    )(*args)


def shifted(x, way):
    nx, ny = lax.axis_size("gx"), lax.axis_size("gy")
    pairs = [
        (((i + way[0]) % nx) * ny + (j + way[1]) % ny, i * ny + j)
        for i in range(nx)
        for j in range(ny)
    ]
    return lax.ppermute(x, ("gx", "gy"), pairs)


def swapped(x):
    count = lax.axis_size("gz")
    return lax.ppermute(x, "gz", [(i, i ^ 1) for i in range(count)])


def per_device(
    positions,
    attributes,
    edge_center,
    edge_other,
    edge_count,
    rim_rows,
    z_rows,
    w_emb,
    w_rbf,
    w_chan,
    w_lat,
    w_ten,
    w_out,
):
    pos = positions[0, 0, 0]
    attr = attributes[0, 0, 0]
    rim = rim_rows[0, 0, 0]
    zr = z_rows[0, 0]
    count = edge_count[0, 0]
    atoms, width = attr.shape
    edges = edge_center.shape[-1]
    features = w_emb.shape[1]
    chans = w_chan.shape[1]
    height = width + PARTS
    inner_len = atoms + 16 * LANES
    table = inner_len + LANES
    hpad = -(-(table // LANES) // 8) * 8
    eb = 512 if edges % 512 == 0 else LANES
    blocks = edges // eb
    centers = edge_center.reshape(blocks, 1, eb)
    others = edge_other.reshape(blocks, 1, eb)
    lift = (1 - 2 * lax.axis_index("gz")).astype(f32).reshape(1)
    big = 60 * 1024 * 1024

    w_emb_t = w_emb.T
    rbf_hi = w_rbf.astype(bf16)
    rbf_lo = (w_rbf - rbf_hi.astype(f32)).astype(bf16)
    w_rad = jnp.concatenate(
        [rbf_hi, rbf_hi, rbf_lo, rbf_lo, jnp.zeros((LANES - 32, features), bf16)], axis=0
    ).T
    w_rbf2 = jnp.concatenate([rbf_hi, rbf_lo], axis=0)
    w_back = jnp.concatenate([w_lat, w_ten], axis=0)
    w_out_col = w_out[:, None]

    shape = jax.ShapeDtypeStruct
    sends = tuple(shape((height, len(routes[way]) * LANES), bf16) for way in directions)
    own, *sent = call(
        pack_kernel,
        (shape((height, atoms), bf16),) + sends,
        (pos, attr, rim),
        [pltpu.VMEM((PARTS, atoms), f32)],
    )
    got = [shifted(x, way) for x, way in zip(sent, directions)]
    inner, slab_send = call(
        slab_kernel,
        (shape((height, inner_len), bf16), shape((height, LANES), bf16)),
        (pos, own, zr, *got),
        [pltpu.VMEM((PARTS, inner_len), f32)],
    )
    slab_got = swapped(slab_send)
    feat, place = call(
        embed_kernel,
        (shape((features, inner_len), bf16), shape((6, hpad, LANES), f32)),
        (inner, w_emb_t),
    )
    grads, energy = call(
        edge_kernel,
        (shape((3, hpad, LANES), f32), shape((8, LANES), f32)),
        (
            count,
            lift,
            centers,
            others,
            feat,
            place,
            slab_got,
            w_emb_t,
            w_rad,
            w_chan.T,
            w_chan,
            w_lat.T,
            w_ten.T,
            w_back,
            w_out_col,
            w_rbf2,
        ),
        [
            pltpu.VMEM((features, table + LANES), bf16),
            pltpu.VMEM((6, hpad, LANES), f32),
            pltpu.VMEM((table + LANES, eb), bf16),
            pltpu.VMEM((blocks, atoms, eb), bf16),
            pltpu.VMEM((blocks, LANES, eb), bf16),
            pltpu.VMEM((blocks, LANES, eb), bf16),
            pltpu.VMEM((blocks, features, eb), bf16),
            pltpu.VMEM((blocks, features, eb), bf16),
            pltpu.VMEM((blocks, chans, eb), f32),
            pltpu.VMEM((blocks, 16, eb), f32),
            pltpu.VMEM((blocks, features, eb), bf16),
            pltpu.VMEM((blocks, 64, eb), f32),
            pltpu.VMEM((9 * chans, atoms), f32),
            pltpu.VMEM((9 * chans, atoms), bf16),
            pltpu.VMEM((9 * chans, atoms), f32),
            pltpu.VMEM((6 * hpad, LANES), f32),
            pltpu.VMEM((64, LANES), f32),
        ],
        smem=2,
        limit=big,
    )
    slab_back = swapped(grads[:, table // LANES - 1])
    messages = tuple(shape((3 * len(routes[way]), LANES), f32) for way in directions)
    own_grad, *sent = call(
        return_kernel,
        (shape((3, 8, LANES), f32),) + messages,
        (grads, slab_back, zr),
    )
    got = [shifted(x, (-way[0], -way[1])) for x, way in zip(sent, directions)]
    forces = call(
        force_kernel,
        shape((3, atoms), f32),
        (own_grad, rim, *got),
        [pltpu.VMEM((8, 8, LANES), f32)],
    )
    atom_energy = energy[0 : atoms // LANES].reshape(1, 1, 1, atoms)
    return (atom_energy, forces[None, None, None])


def solution(mesh):
    return jax.shard_map(
        per_device,
        mesh=mesh,
        in_specs=(
            P("gx", "gy", "gz", None, None),
            P("gx", "gy", "gz", None, None),
            P("gx", "gy", "gz", None),
            P("gx", "gy", "gz", None),
            P("gx", "gy", "gz"),
            P("gx", "gy", "gz", None, None),
            P("gx", "gy", "gz", None),
            P(),
            P(),
            P(),
            P(),
            P(),
            P(),
        ),
        out_specs=(P("gx", "gy", "gz", None), P("gx", "gy", "gz", None, None)),
        check_vma=False,
    )
```

time: 1300 us -> 122 us (0.09); the launches traced: 1280 us -> 122 us
  starting transfers between devices: 606 us -> 26.1 us
  local copies, waits for them, and re-layouts: 336 us -> 12 us
  other arithmetic: 244 us -> 3.03 us
  Pallas kernels: 0 us -> 67.2 us
  matrix products: 64.8 us -> 0 us
    ppermute x10 -> x18, starting transfers between devices: 606 us -> 26.1 us  [the longest x16 24 us: shifted(): return lax.ppermute(x, ('gx', 'gy'), pairs)]
    gather x61 -> x0, local copies, waits for them, and re-layouts: 227 us -> none  [the longest x30 80.4 us: latent_of(): separation = position_table[:, others] - position_table[:, centers]]
    add_any x21 -> x0, other arithmetic: 85.6 us -> none  [the longest x6 78.6 us: latent_of(): separation = position_table[:, others] - position_table[:, centers]]
    scatter-add x11 -> x0, other arithmetic: 81.1 us -> none  [the longest x3 25.1 us: energy_terms(): gathered = tensor[centers]]
    pallas_call x0 -> x6, Pallas kernels: none -> 67.2 us  [call(): pl.pallas_call(kernel, out_shape=out_shape, in_specs=[scalar] * smem + [v...]
    dot_general x37 -> x0, matrix products: 64.8 us -> none  [the longest x15 31.7 us: latent_of(): lax.dot_general(radial, w_rbf, (((0,), (0,)), ((), ())), precision=lax.Pr...]
    while x232 -> x0, local copies, waits for them, and re-layouts: 41 us -> none
    slice x24 -> x1, local copies, waits for them, and re-layouts: 24.1 us -> 1.26 us  [per_device(): atom_energy = energy[0:atoms // LANES].reshape(1, 1, 1, atoms)]
  transfers between devices with their start and end apart: 10 -> 18, of which waited for: 9 -> 5; matrix products, arithmetic and copies ran while one was open for 1% -> 7% of each run, Pallas kernels for 0% -> 2%
where the time goes in v1:
time: 122 us
  Pallas kernels  67.2 us (55%)
  starting transfers between devices  26.1 us (21%)
  local copies, waits for them, and re-layouts  12 us (10%)
  waiting for transfers between devices  11.7 us (10%)
  other arithmetic  3.03 us (2%)
  between operations  1.53 us (1%)
    pallas_call x6, Pallas kernels, call(): pl.pallas_call(kernel, out_shape=out_shape, in_specs=[scalar] * smem + [v...  67.2 us
    ppermute x16, starting transfers between devices, shifted(): return lax.ppermute(x, ('gx', 'gy'), pairs)  24 us
    ppermute x16, waiting for transfers between devices, shifted(): return lax.ppermute(x, ('gx', 'gy'), pairs)  8.65 us
    unnamed x52, local copies, waits for them, and re-layouts  8.12 us
    ppermute x2, waiting for transfers between devices, swapped(): return lax.ppermute(x, 'gz', [(i, i ^ 1) for i in range(count)])  3.04 us
  transfers between devices with their start and end apart: 18, of which 5 were waited for; matrix products, arithmetic and copies ran while one was open for 7% of the time, Pallas kernels for 2%

profile of v1, /device:TPU:0, one launch (start us, length us, event | category | flops | bytes accessed | tf_op | source)
XLA Modules:
  0.0 121.5 jit_solution(13351838987006241908)
XLA Ops:
  0.7 1.4 %copy.38 = f32[1,1,1,3,512]{4,3,2,1,0:T(4,128)} copy(f32[1,1,1,3,512]{4,2,3,1,0:T(1,128)} %param.13) | data formatting | bytes 12288
  2.0 2.2 %shard_map.140 = (bf16[144,512]{1,0:T(8,128)(2,1)}, bf16[144,384]{1,0:T(8,128)(2,1)}, bf16[144,384]{1,0:T(8,128)(2,1)}, bf16[144,384]{1,0:T(8,128)(2,1)}, bf16[1...) custom-call(f32[3,512]{1,0:T(4,128)} %bitcast.28, ...), custom_call_target="tpu_custom_call" | custom-call | tf_op jit(solution)/shard_map/pallas_call | solution.py:423
  4.7 2.6 %collective-permute-start.1 = (bf16[144,384]{1,0:T(8,128)(2,1)}, bf16[144,384]{1,0:T(8,128)(2,1)S(1)}, u32[]{:S(2)}, u32[]{:S(2)}) collective-permute-start(bf16[144,384]{1,0:T(8,128)(2,1)} %get-tuple-element.28), channel_id=1, source_target_pairs={{6,0},{0,2},{2,4},{4,6},{14,8},{8,10},{10,12},{12,14},{22,16},{16,... | collective-permute-start | bytes 331784 | tf_op jit(solution)/shard_map/ppermute | solution.py:440
  7.3 2.5 %collective-permute-start.4 = (bf16[144,128]{1,0:T(8,128)(2,1)}, bf16[144,128]{1,0:T(8,128)(2,1)S(1)}, u32[]{:S(2)}, u32[]{:S(2)}) collective-permute-start(bf16[144,128]{1,0:T(8,128)(2,1)} %get-tuple-element.31), channel_id=1, source_target_pairs={{30,0},{24,2},{26,4},{28,6},{6,8},{0,10},{2,12},{4,14},{14,16},{8,... | collective-permute-start | bytes 110600 | tf_op jit(solution)/shard_map/ppermute | solution.py:440
  9.8 2.0 %collective-permute-start.5 = (bf16[144,128]{1,0:T(8,128)(2,1)}, bf16[144,128]{1,0:T(8,128)(2,1)S(1)}, u32[]{:S(2)}, u32[]{:S(2)}) collective-permute-start(bf16[144,128]{1,0:T(8,128)(2,1)} %get-tuple-element.32), channel_id=1, source_target_pairs={{26,0},{28,2},{30,4},{24,6},{2,8},{4,10},{6,12},{0,14},{10,16},{12... | collective-permute-start | bytes 110600 | tf_op jit(solution)/shard_map/ppermute | solution.py:440
  13.3 1.6 %collective-permute-done.4.rest_4_ = bf16[144,128]{1,0:T(8,128)(2,1)S(1)} collective-permute-done((bf16[144,128]{1,0:T(8,128)(2,1)}, bf16[144,128]{1,0:T(8,128)(2,1)S(1)}, u32[]{:S(2)}, u32[]{:S(2)}) %collective-permute-start.4) | collective-permute-done | bytes 36896 | tf_op jit(solution)/shard_map/ppermute | solution.py:440
  14.9 2.5 %collective-permute-start.2 = (bf16[144,384]{1,0:T(8,128)(2,1)}, bf16[144,384]{1,0:T(8,128)(2,1)S(1)}, u32[]{:S(2)}, u32[]{:S(2)}) collective-permute-start(bf16[144,384]{1,0:T(8,128)(2,1)} %get-tuple-element.29), channel_id=1, source_target_pairs={{2,0},{4,2},{6,4},{0,6},{10,8},{12,10},{14,12},{8,14},{18,16},{20,... | collective-permute-start | bytes 331784 | tf_op jit(solution)/shard_map/ppermute | solution.py:440
  17.4 1.2 collective-permute-start.7
  18.5 1.7 %pad_maximum_fusion.w_back_ref = bf16[448,256]{1,0:T(8,128)(2,1)} fusion(bf16[192,256]{1,0:T(8,128)(2,1)} %param.24, bf16[256,256]{1,0:T(8,128)(2,1)} %param.23), kind=kLoop, calls=%fused_computation | loop fusion | flops 458752 | bytes 458752 | tf_op jit(solution)/shard_map/concatenate | solution.py:490
  21.8 2.3 %shard_map.141 = (bf16[144,2560]{1,0:T(8,128)(2,1)}, bf16[144,128]{1,0:T(8,128)(2,1)}) custom-call(f32[3,512]{1,0:T(4,128)} %bitcast.29, bf16[144,512]{1,0:T(8,128)(2,1)} %get-tuple-element.26.own_ref, s32[1,128]{1,0:T(1,128)} %bitcast.35, bf16[144,384]{1,0:T(8,128)(2,1)} %copy-done.3, bf16[144,384]{1,0:T(8,128)(2,1)} %copy-done.4, ...), custom_call_target="tpu_custom_call" | custom-call | tf_op jit(solution)/shard_map/pallas_call | solution.py:423
  24.1 1.5 %collective-permute-start.8 = (bf16[144,128]{1,0:T(8,128)(2,1)}, bf16[144,128]{1,0:T(8,128)(2,1)S(1)}, u32[]{:S(2)}, u32[]{:S(2)}) collective-permute-start(bf16[144,128]{1,0:T(8,128)(2,1)} %get-tuple-element.38), channel_id=1, source_target_pairs={{0,1},{1,0},{2,3},{3,2},{4,5},{5,4},{6,7},{7,6},{8,9},{9,8},{10,11... | collective-permute-start | bytes 110600 | tf_op jit(solution)/shard_map/ppermute | solution.py:445
  31.7 2.9 %shard_map.142 = (bf16[256,2560]{1,0:T(8,128)(2,1)}, f32[6,24,128]{2,1,0:T(8,128)}) custom-call(bf16[144,2560]{1,0:T(8,128)(2,1)} %get-tuple-element.35.inner_ref, bf16[256,128]{1,0:T(8,128)(2,1)} %bitcast.21), custom_call_target="tpu_custom_call" | custom-call | tf_op jit(solution)/shard_map/pallas_call | solution.py:423
  35.2 56.5 %shard_map.143 = (f32[3,24,128]{2,1,0:T(8,128)}, f32[8,128]{1,0:T(8,128)}) custom-call(s32[1]{0:T(128)} %bitcast.20.count_ref, f32[1]{0:T(128)} %bitcast.1.lift_ref, s32[12,1,512]{2,1,0:T(1,128)} %bitcast.31, s32[12,1,512]{2,1,0:T(1,128)} %bitcast.32, bf16[256,2560]{1,0:T(8,128)(2,1)} %get-tuple-element.36.feat_in_ref, ...), custom_call_target="tpu_custom_call" | custom-call | tf_op jit(solution)/shard_map/pallas_call | solution.py:423
  93.1 3.0 %collective-permute-done.9.back_ref = f32[3,128]{1,0:T(4,128)S(1)} collective-permute-done((f32[3,128]{1,0:T(4,128)S(1)}, f32[3,128]{1,0:T(4,128)S(1)}, u32[]{:S(2)}, u32[]{:S(2)}) %collective-permute-start.9) | collective-permute-done | bytes 1568 | tf_op jit(solution)/shard_map/ppermute | solution.py:445
  96.7 1.6 %shard_map.144 = (f32[3,8,128]{2,1,0:T(8,128)}, f32[9,128]{1,0:T(8,128)}, f32[9,128]{1,0:T(8,128)}, f32[9,128]{1,0:T(8,128)}, f32[9,128]{1,0:T(8,128)}, /*index=...) custom-call(f32[3,24,128]{2,1,0:T(8,128)} %get-tuple-element.40.grad_ref, ...), custom_call_target="tpu_custom_call" | custom-call | tf_op jit(solution)/shard_map/pallas_call | solution.py:423
  98.3 2.8 %collective-permute-start.14 = (f32[3,128]{1,0:T(4,128)}, f32[3,128]{1,0:T(4,128)S(1)}, u32[]{:S(2)}, u32[]{:S(2)}) collective-permute-start(f32[3,128]{1,0:T(4,128)} %get-tuple-element.46), channel_id=1, source_target_pairs={{10,0},{12,2},{14,4},{8,6},{18,8},{20,10},{22,12},{16,14},{26,16},... | collective-permute-start | bytes 4616 | tf_op jit(solution)/shard_map/ppermute | solution.py:440
  101.1 1.5 %collective-permute-start.10 = (f32[9,128]{1,0:T(8,128)}, f32[9,128]{1,0:T(8,128)S(1)}, u32[]{:S(2)}, u32[]{:S(2)}) collective-permute-start(f32[9,128]{1,0:T(8,128)} %get-tuple-element.42), channel_id=1, source_target_pairs={{8,0},{10,2},{12,4},{14,6},{16,8},{18,10},{20,12},{22,14},{24,16},... | collective-permute-start | bytes 13832 | tf_op jit(solution)/shard_map/ppermute | solution.py:440
  102.6 3.4 %collective-permute-start.11 = (f32[9,128]{1,0:T(8,128)}, f32[9,128]{1,0:T(8,128)S(1)}, u32[]{:S(2)}, u32[]{:S(2)}) collective-permute-start(f32[9,128]{1,0:T(8,128)} %get-tuple-element.43), channel_id=1, source_target_pairs={{2,0},{4,2},{6,4},{0,6},{10,8},{12,10},{14,12},{8,14},{18,16},{20,... | collective-permute-start | bytes 13832 | tf_op jit(solution)/shard_map/ppermute | solution.py:440
  106.1 4.3 %collective-permute-start.16 = (f32[3,128]{1,0:T(4,128)}, f32[3,128]{1,0:T(4,128)S(1)}, u32[]{:S(2)}, u32[]{:S(2)}) collective-permute-start(f32[3,128]{1,0:T(4,128)} %get-tuple-element.48), channel_id=1, source_target_pairs={{26,0},{28,2},{30,4},{24,6},{2,8},{4,10},{6,12},{0,14},{10,16},{12... | collective-permute-start | bytes 4616 | tf_op jit(solution)/shard_map/ppermute | solution.py:440
  110.5 1.5 %collective-permute-done.16.rest_6_ = f32[3,128]{1,0:T(4,128)S(1)} collective-permute-done((f32[3,128]{1,0:T(4,128)}, f32[3,128]{1,0:T(4,128)S(1)}, u32[]{:S(2)}, u32[]{:S(2)}) %collective-permute-start.16) | collective-permute-done | bytes 1568 | tf_op jit(solution)/shard_map/ppermute | solution.py:440
  112.0 1.3 %slice.6 = f32[4,128]{1,0:T(4,128)} slice(f32[8,128]{1,0:T(8,128)} %get-tuple-element.39), slice={[0:4], [0:128]} | slice | bytes 4096 | tf_op jit(solution)/shard_map/slice | solution.py:571
  113.2 4.6 %collective-permute-done.17.rest_7_ = f32[3,128]{1,0:T(4,128)S(1)} collective-permute-done((f32[3,128]{1,0:T(4,128)}, f32[3,128]{1,0:T(4,128)S(1)}, u32[]{:S(2)}, u32[]{:S(2)}) %collective-permute-start.17) | collective-permute-done | bytes 1568 | tf_op jit(solution)/shard_map/ppermute | solution.py:440
  118.5 1.7 %shard_map.145 = f32[3,512]{1,0:T(4,128)} custom-call(f32[3,8,128]{2,1,0:T(8,128)} %get-tuple-element.41.own_ref, s32[8,128]{1,0:T(8,128)} %bitcast.34, f32[9,128]{1,0:T(8,128)} %copy-done.13, f32[9,128]{1,0:T(8,128)} %copy-done.14, f32[9,128]{1,0:T(8,128)} %copy-done.15, f32[9,128]{1,0:T(8,128)} %copy-done.16, f32[3,128]{1,0:T(4,128)} %copy-done.17, ...), custom_call_target="tpu_custom_call" | custom-call | tf_op jit(solution)/shard_map/pallas_call | solution.py:423
  120.2 1.3 %copy.35 = f32[1,1,1,3,512]{4,2,3,1,0:T(1,128)} copy(f32[1,1,1,3,512]{4,3,2,1,0:T(4,128)} %bitcast.30) | data formatting | bytes 12288
  (81 shorter events, 12.1 us)
Async XLA Ops:
  0.6 25.8 %copy-start = (bf16[256,256]{1,0:T(8,128)(2,1)S(1)}, bf16[256,256]{1,0:T(8,128)(2,1)}, u32[]{:S(2)}) copy-start(bf16[256,256]{1,0:T(8,128)(2,1)} %param.23) | copy-start | bytes 393220
  0.6 26.6 %copy-start.1 = (bf16[192,256]{1,0:T(8,128)(2,1)S(1)}, bf16[192,256]{1,0:T(8,128)(2,1)}, u32[]{:S(2)}) copy-start(bf16[192,256]{1,0:T(8,128)(2,1)} %param.24) | copy-start | bytes 294916
  0.7 27.3 %copy-start.7 = (bf16[128,256]{1,0:T(8,128)(2,1)S(1)}, bf16[128,256]{1,0:T(8,128)(2,1)}, u32[]{:S(2)}) copy-start(bf16[128,256]{1,0:T(8,128)(2,1)} %param.20) | copy-start | bytes 196612
  0.7 28.0 %copy-start.22 = (f32[256]{0:T(256)S(1)}, f32[256]{0:T(256)}, u32[]{:S(2)}) copy-start(f32[256]{0:T(256)} %param.25) | copy-start | bytes 3076
  0.7 28.8 %copy-start.2 = (bf16[256,64]{0,1:T(8,128)(2,1)S(1)}, bf16[256,64]{0,1:T(8,128)(2,1)}, u32[]{:S(2)}) copy-start(bf16[256,64]{0,1:T(8,128)(2,1)} %param.22) | copy-start | bytes 98308
  4.3 16.8 %collective-permute-start = (bf16[144,384]{1,0:T(8,128)(2,1)}, bf16[144,384]{1,0:T(8,128)(2,1)S(1)}, u32[]{:S(2)}, u32[]{:S(2)}) collective-permute-start(bf16[144,384]{1,0:T(8,128)(2,1)} %get-tuple-element.27), channel_id=1, source_target_pairs={{24,0},{26,2},{28,4},{30,6},{0,8},{2,10},{4,12},{6,14},{8,16},{10,... | collective-permute-start | bytes 331784 | tf_op jit(solution)/shard_map/ppermute | solution.py:440
  4.7 16.3 %collective-permute-start.1 = (bf16[144,384]{1,0:T(8,128)(2,1)}, bf16[144,384]{1,0:T(8,128)(2,1)S(1)}, u32[]{:S(2)}, u32[]{:S(2)}) collective-permute-start(bf16[144,384]{1,0:T(8,128)(2,1)} %get-tuple-element.28), channel_id=1, source_target_pairs={{6,0},{0,2},{2,4},{4,6},{14,8},{8,10},{10,12},{12,14},{22,16},{16,... | collective-permute-start | bytes 331784 | tf_op jit(solution)/shard_map/ppermute | solution.py:440
  7.3 7.5 %collective-permute-start.4 = (bf16[144,128]{1,0:T(8,128)(2,1)}, bf16[144,128]{1,0:T(8,128)(2,1)S(1)}, u32[]{:S(2)}, u32[]{:S(2)}) collective-permute-start(bf16[144,128]{1,0:T(8,128)(2,1)} %get-tuple-element.31), channel_id=1, source_target_pairs={{30,0},{24,2},{26,4},{28,6},{6,8},{0,10},{2,12},{4,14},{14,16},{8,... | collective-permute-start | bytes 110600 | tf_op jit(solution)/shard_map/ppermute | solution.py:440
  9.8 7.5 %collective-permute-start.5 = (bf16[144,128]{1,0:T(8,128)(2,1)}, bf16[144,128]{1,0:T(8,128)(2,1)S(1)}, u32[]{:S(2)}, u32[]{:S(2)}) collective-permute-start(bf16[144,128]{1,0:T(8,128)(2,1)} %get-tuple-element.32), channel_id=1, source_target_pairs={{26,0},{28,2},{30,4},{24,6},{2,8},{4,10},{6,12},{0,14},{10,16},{12... | collective-permute-start | bytes 110600 | tf_op jit(solution)/shard_map/ppermute | solution.py:440
  11.8 5.5 %collective-permute-start.6 = (bf16[144,128]{1,0:T(8,128)(2,1)}, bf16[144,128]{1,0:T(8,128)(2,1)S(1)}, u32[]{:S(2)}, u32[]{:S(2)}) collective-permute-start(bf16[144,128]{1,0:T(8,128)(2,1)} %get-tuple-element.33), channel_id=1, source_target_pairs={{14,0},{8,2},{10,4},{12,6},{22,8},{16,10},{18,12},{20,14},{30,16},... | collective-permute-start | bytes 110600 | tf_op jit(solution)/shard_map/ppermute | solution.py:440
  14.9 6.2 %collective-permute-start.2 = (bf16[144,384]{1,0:T(8,128)(2,1)}, bf16[144,384]{1,0:T(8,128)(2,1)S(1)}, u32[]{:S(2)}, u32[]{:S(2)}) collective-permute-start(bf16[144,384]{1,0:T(8,128)(2,1)} %get-tuple-element.29), channel_id=1, source_target_pairs={{2,0},{4,2},{6,4},{0,6},{10,8},{12,10},{14,12},{8,14},{18,16},{20,... | collective-permute-start | bytes 331784 | tf_op jit(solution)/shard_map/ppermute | solution.py:440
  17.4 3.7 %collective-permute-start.3 = (bf16[144,384]{1,0:T(8,128)(2,1)}, bf16[144,384]{1,0:T(8,128)(2,1)S(1)}, u32[]{:S(2)}, u32[]{:S(2)}) collective-permute-start(bf16[144,384]{1,0:T(8,128)(2,1)} %get-tuple-element.30), channel_id=1, source_target_pairs={{8,0},{10,2},{12,4},{14,6},{16,8},{18,10},{20,12},{22,14},{24,16},... | collective-permute-start | bytes 331784 | tf_op jit(solution)/shard_map/ppermute | solution.py:440
  17.4 3.6 %collective-permute-start.7 = (bf16[144,128]{1,0:T(8,128)(2,1)}, bf16[144,128]{1,0:T(8,128)(2,1)S(1)}, u32[]{:S(2)}, u32[]{:S(2)}) collective-permute-start(bf16[144,128]{1,0:T(8,128)(2,1)} %get-tuple-element.34), channel_id=1, source_target_pairs={{10,0},{12,2},{14,4},{8,6},{18,8},{20,10},{22,12},{16,14},{26,16},... | collective-permute-start | bytes 110600 | tf_op jit(solution)/shard_map/ppermute | solution.py:440
  24.1 10.5 %collective-permute-start.8 = (bf16[144,128]{1,0:T(8,128)(2,1)}, bf16[144,128]{1,0:T(8,128)(2,1)S(1)}, u32[]{:S(2)}, u32[]{:S(2)}) collective-permute-start(bf16[144,128]{1,0:T(8,128)(2,1)} %get-tuple-element.38), channel_id=1, source_target_pairs={{0,1},{1,0},{2,3},{3,2},{4,5},{5,4},{6,7},{7,6},{8,9},{9,8},{10,11... | collective-permute-start | bytes 110600 | tf_op jit(solution)/shard_map/ppermute | solution.py:445
  92.5 3.7 %collective-permute-start.9 = (f32[3,128]{1,0:T(4,128)S(1)}, f32[3,128]{1,0:T(4,128)S(1)}, u32[]{:S(2)}, u32[]{:S(2)}) collective-permute-start(f32[3,128]{1,0:T(4,128)S(1)} %slice_bitcast_fusion), channel_id=1, source_target_pairs={{0,1},{1,0},{2,3},{3,2},{4,5},{5,4},{6,7},{7,6},{8,9},{9,8},{10,11... | collective-permute-start | bytes 4616 | tf_op jit(solution)/shard_map/ppermute | solution.py:445
  98.3 7.7 %collective-permute-start.14 = (f32[3,128]{1,0:T(4,128)}, f32[3,128]{1,0:T(4,128)S(1)}, u32[]{:S(2)}, u32[]{:S(2)}) collective-permute-start(f32[3,128]{1,0:T(4,128)} %get-tuple-element.46), channel_id=1, source_target_pairs={{10,0},{12,2},{14,4},{8,6},{18,8},{20,10},{22,12},{16,14},{26,16},... | collective-permute-start | bytes 4616 | tf_op jit(solution)/shard_map/ppermute | solution.py:440
  101.1 5.1 %collective-permute-start.15 = (f32[3,128]{1,0:T(4,128)}, f32[3,128]{1,0:T(4,128)S(1)}, u32[]{:S(2)}, u32[]{:S(2)}) collective-permute-start(f32[3,128]{1,0:T(4,128)} %get-tuple-element.47), channel_id=1, source_target_pairs={{14,0},{8,2},{10,4},{12,6},{22,8},{16,10},{18,12},{20,14},{30,16},... | collective-permute-start | bytes 4616 | tf_op jit(solution)/shard_map/ppermute | solution.py:440
  101.1 16.8 %collective-permute-start.10 = (f32[9,128]{1,0:T(8,128)}, f32[9,128]{1,0:T(8,128)S(1)}, u32[]{:S(2)}, u32[]{:S(2)}) collective-permute-start(f32[9,128]{1,0:T(8,128)} %get-tuple-element.42), channel_id=1, source_target_pairs={{8,0},{10,2},{12,4},{14,6},{16,8},{18,10},{20,12},{22,14},{24,16},... | collective-permute-start | bytes 13832 | tf_op jit(solution)/shard_map/ppermute | solution.py:440
  102.6 15.3 %collective-permute-start.11 = (f32[9,128]{1,0:T(8,128)}, f32[9,128]{1,0:T(8,128)S(1)}, u32[]{:S(2)}, u32[]{:S(2)}) collective-permute-start(f32[9,128]{1,0:T(8,128)} %get-tuple-element.43), channel_id=1, source_target_pairs={{2,0},{4,2},{6,4},{0,6},{10,8},{12,10},{14,12},{8,14},{18,16},{20,... | collective-permute-start | bytes 13832 | tf_op jit(solution)/shard_map/ppermute | solution.py:440
  106.0 11.9 %collective-permute-start.12 = (f32[9,128]{1,0:T(8,128)}, f32[9,128]{1,0:T(8,128)S(1)}, u32[]{:S(2)}, u32[]{:S(2)}) collective-permute-start(f32[9,128]{1,0:T(8,128)} %get-tuple-element.44), channel_id=1, source_target_pairs={{6,0},{0,2},{2,4},{4,6},{14,8},{8,10},{10,12},{12,14},{22,16},{16,... | collective-permute-start | bytes 13832 | tf_op jit(solution)/shard_map/ppermute | solution.py:440
  106.0 11.9 %copy-start.17 = (f32[3,128]{1,0:T(4,128)}, f32[3,128]{1,0:T(4,128)S(1)}, u32[]{:S(2)}) copy-start(f32[3,128]{1,0:T(4,128)S(1)} %collective-permute-done.14.rest_4_) | copy-start | bytes 4612
  106.1 11.9 %collective-permute-start.13 = (f32[9,128]{1,0:T(8,128)}, f32[9,128]{1,0:T(8,128)S(1)}, u32[]{:S(2)}, u32[]{:S(2)}) collective-permute-start(f32[9,128]{1,0:T(8,128)} %get-tuple-element.45), channel_id=1, source_target_pairs={{24,0},{26,2},{28,4},{30,6},{0,8},{2,10},{4,12},{6,14},{8,16},{10,... | collective-permute-start | bytes 13832 | tf_op jit(solution)/shard_map/ppermute | solution.py:440
  106.1 5.8 %collective-permute-start.16 = (f32[3,128]{1,0:T(4,128)}, f32[3,128]{1,0:T(4,128)S(1)}, u32[]{:S(2)}, u32[]{:S(2)}) collective-permute-start(f32[3,128]{1,0:T(4,128)} %get-tuple-element.48), channel_id=1, source_target_pairs={{26,0},{28,2},{30,4},{24,6},{2,8},{4,10},{6,12},{0,14},{10,16},{12... | collective-permute-start | bytes 4616 | tf_op jit(solution)/shard_map/ppermute | solution.py:440
  112.0 5.9 %collective-permute-start.17 = (f32[3,128]{1,0:T(4,128)}, f32[3,128]{1,0:T(4,128)S(1)}, u32[]{:S(2)}, u32[]{:S(2)}) collective-permute-start(f32[3,128]{1,0:T(4,128)} %get-tuple-element.49), channel_id=1, source_target_pairs={{30,0},{24,2},{26,4},{28,6},{6,8},{0,10},{2,12},{4,14},{14,16},{8,... | collective-permute-start | bytes 4616 | tf_op jit(solution)/shard_map/ppermute | solution.py:440
  (17 other events, 39.1 us)

commit v2 on v1

--- a/solution.py
+++ b/solution.py
@@ -28,7 +28,7 @@
 for _cycle, (_p, _q) in enumerate(cycle_cells):
     (_sx, _a), (_sy, _b) = source_of(_p), source_of(_q)
     routes.setdefault((_sx, _sy), []).append((_cycle, rim_cells.index((_a, _b))))
-directions = sorted(routes, key=lambda way: (-len(routes[way]), way))
+sides = [(0, -1), (0, 1), (-1, 0), (1, 0)]
 
 
 def dot(a, b):
@@ -69,47 +69,100 @@
         rows_of((width, width)) == lax.broadcasted_iota(jnp.int32, (width, width), 1), 1.0, 0.0
     ).astype(bf16)
     own_ref[0:width, :] = dot_t(eye, attr_ref[...]).astype(bf16)
-    upper, lower = halves(pos_ref[...])
     parts[...] = jnp.zeros_like(parts)
-    parts[0:3, :] = upper
-    parts[3:6, :] = lower
+    for d in range(3):
+        parts[d : d + 1, :], parts[3 + d : 4 + d, :] = halves(pos_ref[d])
     own_ref[width : width + PARTS, :] = parts[...].astype(bf16)
     packed = own_ref[...]
     for rim in range(8):
         hot = one_hot(rim_ref[rim : rim + 1, :], atoms).astype(bf16)
         cell = dot(packed, hot).astype(bf16)
-        for way, send in zip(directions, sends):
+        for way, send in zip(sides, sends):
             for slot, (_, source) in enumerate(routes[way]):
                 if source == rim:
                     send[:, slot * LANES : (slot + 1) * LANES] = cell
 
 
+def corner_kernel(minus_ref, plus_ref, to_plus_ref, to_minus_ref):
+    first, last = slice(0, LANES), slice(2 * LANES, 3 * LANES)
+    for slot, ref in enumerate((minus_ref, plus_ref)):
+        lanes = slice(slot * LANES, (slot + 1) * LANES)
+        to_plus_ref[:, lanes] = ref[:, last]
+        to_minus_ref[:, lanes] = ref[:, first]
+
+
 def slab_kernel(pos_ref, own_ref, zrows_ref, *rest):
-    got, (inner_ref, send_ref, parts) = rest[:8], rest[8:]
+    got, corners, (inner_ref, send_ref, parts) = rest[:4], rest[4:6], rest[6:]
     atoms = own_ref.shape[1]
     height = own_ref.shape[0]
     width = height - PARTS
     inner_len = inner_ref.shape[1]
     inner_ref[:, 0:atoms] = own_ref[...]
     parts[...] = jnp.zeros_like(parts)
-    upper, lower = halves(pos_ref[...])
-    parts[0:3, 0:atoms] = upper
-    parts[3:6, 0:atoms] = lower
-    for way, ref in zip(directions, got):
+    for d in range(3):
+        parts[d : d + 1, 0:atoms], parts[3 + d : 4 + d, 0:atoms] = halves(pos_ref[d])
+    arrivals = []
+    for way, ref in zip(sides, got):
         for slot, (cycle, _) in enumerate(routes[way]):
-            lanes = slice(slot * LANES, (slot + 1) * LANES)
-            into = slice(atoms + cycle * LANES, atoms + (cycle + 1) * LANES)
-            inner_ref[0:width, into] = ref[0:width, lanes]
-            arrived = ref[width:height, lanes].astype(f32)
-            joined = arrived[0:3] + arrived[3:6]
-            axis = rows_of((3, LANES))
-            shift = jnp.where(axis == 0, float(way[0]), jnp.where(axis == 1, float(way[1]), 0.0))
-            upper, lower = halves(joined + shift)
-            parts[0:3, into] = upper
-            parts[3:6, into] = lower
+            arrivals.append((way, ref, slot, cycle))
+    for sx, ref in zip((-1, 1), corners):
+        for slot, sy in enumerate((-1, 1)):
+            arrivals.append(((sx, sy), ref, slot, routes[(sx, sy)][0][0]))
+    for way, ref, slot, cycle in arrivals:
+        lanes = slice(slot * LANES, (slot + 1) * LANES)
+        into = slice(atoms + cycle * LANES, atoms + (cycle + 1) * LANES)
+        inner_ref[0:width, into] = ref[0:width, lanes]
+        arrived = ref[width:height, lanes].astype(f32)
+        joined = arrived[0:3] + arrived[3:6]
+        axis = rows_of((3, LANES))
+        shift = jnp.where(axis == 0, float(way[0]), jnp.where(axis == 1, float(way[1]), 0.0))
+        upper, lower = halves(joined + shift)
+        parts[0:3, into] = upper
+        parts[3:6, into] = lower
     inner_ref[width:height, :] = parts[...].astype(bf16)
     hot = one_hot(zrows_ref[...], inner_len).astype(bf16)
     send_ref[...] = dot(inner_ref[...], hot).astype(bf16)
+
+
+def unit(size):
+    lanes = lax.broadcasted_iota(jnp.int32, (size, size), 1)
+    return jnp.where(rows_of((size, size)) == lanes, 1.0, 0.0)
+
+
+def weights_kernel(
+    w_emb_ref,
+    w_rbf_ref,
+    w_chan_t_ref,
+    w_lat_ref,
+    w_ten_ref,
+    w_out_ref,
+    emb_t_ref,
+    rad_ref,
+    chan_ref,
+    lat_t_ref,
+    ten_t_ref,
+    back_ref,
+    out_ref,
+    rbf_ref,
+    scratch,
+):
+    features = w_lat_ref.shape[0]
+    eye = unit(features)
+    eye_b = eye.astype(bf16)
+    emb_t_ref[...] = dot_t(eye_b, w_emb_ref[...]).astype(bf16)
+    chan_ref[...] = dot_t(eye_b, w_chan_t_ref[...]).astype(bf16)
+    lat_t_ref[...] = dot_t(eye_b, w_lat_ref[...]).astype(bf16)
+    ten_t_ref[...] = dot_t(eye_b, w_ten_ref[...]).astype(bf16)
+    back_ref[0:features, :] = w_lat_ref[...]
+    back_ref[features:, :] = w_ten_ref[...]
+    column = jnp.sum(eye * w_out_ref[...], axis=1, keepdims=True)
+    out_ref[...] = jnp.broadcast_to(column, out_ref.shape)
+    upper, lower = halves(w_rbf_ref[...])
+    rbf_ref[...] = jnp.concatenate([upper, lower], axis=0).astype(bf16)
+    scratch[...] = jnp.zeros_like(scratch)
+    for start, value in ((0, upper), (8, upper), (16, lower), (24, lower)):
+        scratch[start : start + 8, :] = value
+    rad_ref[...] = dot_t(eye_b, scratch[...].astype(bf16)).astype(bf16)
 
 
 def embed_kernel(inner_ref, w_emb_ref, feat_ref, place_ref):
@@ -160,6 +213,7 @@
     w_out_ref,
     w_rbf_ref,
     grad_ref,
+    slab_grad_ref,
     energy_ref,
     feat,
     place,
@@ -289,7 +343,7 @@
         pre = dot(w_lat_t_ref[...], latent_s[b]) + dot(w_ten_t_ref[...], invariant)
         s = sigmoid(pre)
         value = pre * s
-        weight = w_out_ref[...]
+        weight = jnp.concatenate([w_out_ref[...]] * (eb // LANES), axis=1)
         summed = jnp.sum(value * weight, axis=0, keepdims=True)
         geo_s[b, 8:9, :] = summed
         dpre = (weight * (env * live) * (s + value * (1.0 - s))).astype(bf16)
@@ -369,10 +423,13 @@
     for d in range(3):
         grad_ref[d] = sum_o[d * hpad : (d + 1) * hpad]
         grad_ref[d, 0:8, :] = sum_o[d * hpad : d * hpad + 8] - sum_c[d * 8 : (d + 1) * 8]
-    energy_ref[...] = sum_c[24:32]
-
-
-def return_kernel(grad_ref, back_ref, zrows_ref, own_ref, *sends):
+        slab_grad_ref[d : d + 1, :] = sum_o[d * hpad + highs - 1 : d * hpad + highs]
+    for high in range(c_highs):
+        lanes = slice(high * LANES, (high + 1) * LANES)
+        energy_ref[:, lanes] = sum_c[24 + high : 25 + high]
+
+
+def return_kernel(grad_ref, back_ref, zrows_ref, own_ref, to_xm_ref, to_xp_ref, to_ym_ref, to_yp_ref):
     hpad = grad_ref.shape[1]
     z_rows = zrows_ref[...]
     mask = one_hot(lax.shift_right_logical(z_rows, 7), hpad)
@@ -387,18 +444,33 @@
     for d in range(3):
         total = grad_ref[d] + landed[d * hpad : (d + 1) * hpad]
         own_ref[d] = total[0:8]
-        for way, send in zip(directions, sends):
-            for slot, (cycle, _) in enumerate(routes[way]):
-                row = base + cycle
-                send[slot * 3 + d : slot * 3 + d + 1, :] = total[row : row + 1]
-
-
-def force_kernel(own_ref, rim_ref, *rest):
-    got, (out_ref, rim_sum) = rest[:8], rest[8:]
+        for cycle, (p, q) in enumerate(cycle_cells):
+            value = total[base + cycle : base + cycle + 1]
+            if p in (0, 4):
+                ref = to_xm_ref if p == 0 else to_xp_ref
+                ref[q * 3 + d : q * 3 + d + 1, :] = value
+            else:
+                ref = to_ym_ref if q == 0 else to_yp_ref
+                ref[(p - 1) * 3 + d : (p - 1) * 3 + d + 1, :] = value
+
+
+def turn_kernel(from_xp_ref, from_xm_ref, to_ym_ref, to_yp_ref, send_ym_ref, send_yp_ref):
+    for q, old, new in ((0, to_ym_ref, send_ym_ref), (4, to_yp_ref, send_yp_ref)):
+        new[0:3, :] = old[0:3, :] + from_xm_ref[q * 3 : q * 3 + 3, :]
+        new[3:6, :] = old[3:6, :]
+        new[6:9, :] = old[6:9, :] + from_xp_ref[q * 3 : q * 3 + 3, :]
+
+
+def force_kernel(
+    own_ref, rim_ref, from_xp_ref, from_xm_ref, from_yp_ref, from_ym_ref, out_ref, rim_sum
+):
     rim_sum[...] = jnp.zeros_like(rim_sum)
-    for way, ref in zip(directions, got):
-        for slot, (_, rim) in enumerate(routes[way]):
-            rim_sum[rim, 0:3, :] += ref[slot * 3 : slot * 3 + 3, :]
+    for a, ref in ((2, from_xp_ref), (0, from_xm_ref)):
+        for b in range(3):
+            rim_sum[rim_cells.index((a, b)), 0:3, :] += ref[(b + 1) * 3 : (b + 2) * 3, :]
+    for b, ref in ((2, from_yp_ref), (0, from_ym_ref)):
+        for a in range(3):
+            rim_sum[rim_cells.index((a, b)), 0:3, :] += ref[a * 3 : (a + 1) * 3, :]
     total = jnp.zeros((48, LANES), f32)
     for rim in range(8):
         index = rim_ref[rim : rim + 1, :]
@@ -412,9 +484,9 @@
         total = total + dot_t(rows, low)
     total = total[0:24] + total[24:48]
     for d in range(3):
-        for high in range(out_ref.shape[1] // LANES):
+        for high in range(out_ref.shape[2] // LANES):
             value = own_ref[d, high : high + 1, :] + total[d * 8 + high : d * 8 + high + 1, :]
-            out_ref[d : d + 1, high * LANES : (high + 1) * LANES] = -value
+            out_ref[d, :, high * LANES : (high + 1) * LANES] = -value
 
 
 def call(kernel, out_shape, args, scratch=(), smem=0, limit=None):
@@ -430,14 +502,9 @@
     )(*args)
 
 
-def shifted(x, way):
-    nx, ny = lax.axis_size("gx"), lax.axis_size("gy")
-    pairs = [
-        (((i + way[0]) % nx) * ny + (j + way[1]) % ny, i * ny + j)
-        for i in range(nx)
-        for j in range(ny)
-    ]
-    return lax.ppermute(x, ("gx", "gy"), pairs)
+def shifted(x, axis, step):
+    count = lax.axis_size(axis)
+    return lax.ppermute(x, axis, [((i + step) % count, i) for i in range(count)])
 
 
 def swapped(x):
@@ -460,7 +527,7 @@
     w_ten,
     w_out,
 ):
-    pos = positions[0, 0, 0]
+    pos = positions.reshape(3, 1, -1)
     attr = attributes[0, 0, 0]
     rim = rim_rows[0, 0, 0]
     zr = z_rows[0, 0]
@@ -478,31 +545,46 @@
     centers = edge_center.reshape(blocks, 1, eb)
     others = edge_other.reshape(blocks, 1, eb)
     lift = (1 - 2 * lax.axis_index("gz")).astype(f32).reshape(1)
-    big = 60 * 1024 * 1024
-
-    w_emb_t = w_emb.T
-    rbf_hi = w_rbf.astype(bf16)
-    rbf_lo = (w_rbf - rbf_hi.astype(f32)).astype(bf16)
-    w_rad = jnp.concatenate(
-        [rbf_hi, rbf_hi, rbf_lo, rbf_lo, jnp.zeros((LANES - 32, features), bf16)], axis=0
-    ).T
-    w_rbf2 = jnp.concatenate([rbf_hi, rbf_lo], axis=0)
-    w_back = jnp.concatenate([w_lat, w_ten], axis=0)
-    w_out_col = w_out[:, None]
+    big = 44 * 1024 * 1024
 
     shape = jax.ShapeDtypeStruct
-    sends = tuple(shape((height, len(routes[way]) * LANES), bf16) for way in directions)
+    w_chan_t = w_chan.T
+    prepared = call(
+        weights_kernel,
+        (
+            shape((features, width), bf16),
+            shape((features, LANES), bf16),
+            shape((features, chans), bf16),
+            shape((features, features), bf16),
+            shape((features, 3 * chans), bf16),
+            shape((features + 3 * chans, features), bf16),
+            shape((features, LANES), f32),
+            shape((16, features), bf16),
+        ),
+        (w_emb, w_rbf, w_chan_t, w_lat, w_ten, w_out[None]),
+        [pltpu.VMEM((LANES, features), f32)],
+    )
     own, *sent = call(
         pack_kernel,
-        (shape((height, atoms), bf16),) + sends,
+        (shape((height, atoms), bf16),) + (shape((height, 3 * LANES), bf16),) * 4,
         (pos, attr, rim),
         [pltpu.VMEM((PARTS, atoms), f32)],
     )
-    got = [shifted(x, way) for x, way in zip(sent, directions)]
+    got = [
+        shifted(x, "gx" if way[0] else "gy", way[0] + way[1]) for x, way in zip(sent, sides)
+    ]
+    to_plus, to_minus = call(
+        corner_kernel,
+        (shape((height, 2 * LANES), bf16),) * 2,
+        (got[0], got[1]),
+    )
+    corners = [shifted(to_plus, "gx", -1), shifted(to_minus, "gx", 1)]
+    corners, prepared = lax.optimization_barrier((corners, prepared))
+    w_emb_t, w_rad, w_chan_r, w_lat_t, w_ten_t, w_back, w_out_col, w_rbf2 = prepared
     inner, slab_send = call(
         slab_kernel,
         (shape((height, inner_len), bf16), shape((height, LANES), bf16)),
-        (pos, own, zr, *got),
+        (pos, own, zr, *got, *corners),
         [pltpu.VMEM((PARTS, inner_len), f32)],
     )
     slab_got = swapped(slab_send)
@@ -511,9 +593,9 @@
         (shape((features, inner_len), bf16), shape((6, hpad, LANES), f32)),
         (inner, w_emb_t),
     )
-    grads, energy = call(
+    grads, slab_grad, energy = call(
         edge_kernel,
-        (shape((3, hpad, LANES), f32), shape((8, LANES), f32)),
+        (shape((3, hpad, LANES), f32), shape((3, LANES), f32), shape((1, atoms), f32)),
         (
             count,
             lift,
@@ -524,10 +606,10 @@
             slab_got,
             w_emb_t,
             w_rad,
-            w_chan.T,
-            w_chan,
-            w_lat.T,
-            w_ten.T,
+            w_chan_t,
+            w_chan_r,
+            w_lat_t,
+            w_ten_t,
             w_back,
             w_out_col,
             w_rbf2,
@@ -554,22 +636,23 @@
         smem=2,
         limit=big,
     )
-    slab_back = swapped(grads[:, table // LANES - 1])
-    messages = tuple(shape((3 * len(routes[way]), LANES), f32) for way in directions)
-    own_grad, *sent = call(
+    slab_back = swapped(slab_grad)
+    along_x, along_y = shape((15, LANES), f32), shape((9, LANES), f32)
+    own_grad, to_xm, to_xp, to_ym, to_yp = call(
         return_kernel,
-        (shape((3, 8, LANES), f32),) + messages,
+        (shape((3, 8, LANES), f32), along_x, along_x, along_y, along_y),
         (grads, slab_back, zr),
     )
-    got = [shifted(x, (-way[0], -way[1])) for x, way in zip(sent, directions)]
+    from_xp, from_xm = shifted(to_xm, "gx", 1), shifted(to_xp, "gx", -1)
+    to_ym, to_yp = call(turn_kernel, (along_y, along_y), (from_xp, from_xm, to_ym, to_yp))
+    from_yp, from_ym = shifted(to_ym, "gy", 1), shifted(to_yp, "gy", -1)
     forces = call(
         force_kernel,
-        shape((3, atoms), f32),
-        (own_grad, rim, *got),
+        shape((3, 1, atoms), f32),
+        (own_grad, rim, from_xp, from_xm, from_yp, from_ym),
         [pltpu.VMEM((8, 8, LANES), f32)],
     )
-    atom_energy = energy[0 : atoms // LANES].reshape(1, 1, 1, atoms)
-    return (atom_energy, forces[None, None, None])
+    return (energy.reshape(1, 1, 1, atoms), forces.reshape(1, 1, 1, 3, atoms))
 
 
 def solution(mesh):

time: 122 us -> 108 us (0.89)
  starting transfers between devices: 26.1 us -> 14.1 us
  local copies, waits for them, and re-layouts: 12 us -> 5.95 us
  Pallas kernels: 67.2 us -> 70.8 us
  waiting for transfers between devices: 11.7 us -> 15 us
  other arithmetic: 3.03 us -> 0 us
    ppermute x16 -> x10, starting transfers between devices: 24 us -> 12 us  [shifted(): lax.ppermute(x, axis, [((i + step) % count, i) for i in range(count)])]
    pallas_call x6 -> x9, Pallas kernels: 67.2 us -> 70.8 us  [call(): pl.pallas_call(kernel, out_shape=out_shape, in_specs=[scalar] * smem + [v...]
    ppermute x16 -> x10, waiting for transfers between devices: 8.65 us -> 12 us  [shifted(): lax.ppermute(x, axis, [((i + step) % count, i) for i in range(count)])]
    concatenate x2 -> x0, other arithmetic: 2.25 us -> none  [the longest x1 1.66 us: per_device(): w_back = jnp.concatenate([w_lat, w_ten], axis=0)]
    unnamed x52 -> x50, local copies, waits for them, and re-layouts: 8.12 us -> 5.95 us
    slice x1 -> x0, local copies, waits for them, and re-layouts: 1.26 us -> none  [per_device(): atom_energy = energy[0:atoms // LANES].reshape(1, 1, 1, atoms)]
  transfers between devices with their start and end apart: 18 -> 12, of which waited for: 5 -> 7; matrix products, arithmetic and copies ran while one was open for 7% -> 0% of each run, Pallas kernels for 2% -> 6%
where the time goes in v2:
time: 108 us; the launch traced here: 107 us
  Pallas kernels  70.8 us (66%)
  waiting for transfers between devices  15 us (14%)
  starting transfers between devices  14.1 us (13%)
  local copies, waits for them, and re-layouts  5.95 us (6%)
  between operations  1.54 us (1%)
    pallas_call x9, Pallas kernels, call(): pl.pallas_call(kernel, out_shape=out_shape, in_specs=[scalar] * smem + [v...  70.8 us
    ppermute x10, starting transfers between devices, shifted(): lax.ppermute(x, axis, [((i + step) % count, i) for i in range(count)])  12 us
    ppermute x10, waiting for transfers between devices, shifted(): lax.ppermute(x, axis, [((i + step) % count, i) for i in range(count)])  12 us
    unnamed x50, local copies, waits for them, and re-layouts  5.95 us
    ppermute x2, waiting for transfers between devices, swapped(): return lax.ppermute(x, 'gz', [(i, i ^ 1) for i in range(count)])  2.97 us
  transfers between devices with their start and end apart: 12, of which 7 were waited for; matrix products, arithmetic and copies ran while one was open for 0% of the time, Pallas kernels for 6%

profile of v2, /device:TPU:0, one launch (start us, length us, event | category | flops | bytes accessed | tf_op | source)
XLA Modules:
  0.0 107.4 jit_solution(16744740571837972752)
XLA Ops:
  0.7 2.3 %shard_map.140 = (bf16[144,512]{1,0:T(8,128)(2,1)}, bf16[144,384]{1,0:T(8,128)(2,1)}, bf16[144,384]{1,0:T(8,128)(2,1)}, bf16[144,384]{1,0:T(8,128)(2,1)}, bf16[144,384]{1,0:T(8,128)(2,1)}) custom-call(f32[3,1,512]{2,1,0:T(1,128)} %bitcast.20, bf16[512,128]{1,0:T(8,128)(2,1)} %bitcast.19, s32[8,128]{1,0:T(8,128)} %bitcast.22), custom_call_target="tpu_custom_call" | custom-call | tf_op jit(solution)/shard_map/pallas_call | solution.py:495
  3.0 3.0 %collective-permute-start = (bf16[144,384]{1,0:T(8,128)(2,1)}, bf16[144,384]{1,0:T(8,128)(2,1)S(1)}, u32[]{:S(2)}, u32[]{:S(2)}) collective-permute-start(bf16[144,384]{1,0:T(8,128)(2,1)} %get-tuple-element.42), channel_id=1, source_target_pairs={{6,0},{0,2},{2,4},{4,6},{7,1},{1,3},{3,5},{5,7},{14,8},{8,10},{10,... | collective-permute-start | bytes 331784 | tf_op jit(solution)/shard_map/ppermute | solution.py:507
  6.0 2.0 %collective-permute-start.1 = (bf16[144,384]{1,0:T(8,128)(2,1)}, bf16[144,384]{1,0:T(8,128)(2,1)S(1)}, u32[]{:S(2)}, u32[]{:S(2)}) collective-permute-start(bf16[144,384]{1,0:T(8,128)(2,1)} %get-tuple-element.43), channel_id=1, source_target_pairs={{2,0},{4,2},{6,4},{0,6},{3,1},{5,3},{7,5},{1,7},{10,8},{12,10},{14... | collective-permute-start | bytes 331784 | tf_op jit(solution)/shard_map/ppermute | solution.py:507
  8.0 1.8 %collective-permute-start.3 = (bf16[144,384]{1,0:T(8,128)(2,1)}, bf16[144,384]{1,0:T(8,128)(2,1)S(1)}, u32[]{:S(2)}, u32[]{:S(2)}) collective-permute-start(bf16[144,384]{1,0:T(8,128)(2,1)} %get-tuple-element.45), channel_id=1, source_target_pairs={{8,0},{16,8},{24,16},{0,24},{9,1},{17,9},{25,17},{1,25},{10,2},{18... | collective-permute-start | bytes 331784 | tf_op jit(solution)/shard_map/ppermute | solution.py:507
  9.8 2.3 %collective-permute-done.minus_ref.rest_0_ = bf16[144,384]{1,0:T(8,128)(2,1)S(1)} collective-permute-done((bf16[144,384]{1,0:T(8,128)(2,1)}, bf16[144,384]{1,0:T(8,128)(2,1)S(1)}, u32[]{:S(2)}, u32[]{:S(2)}) %collective-permute-start) | collective-permute-done | bytes 110624 | tf_op jit(solution)/shard_map/ppermute | solution.py:507
  12.1 1.0 collective-permute-done.1.plus_ref.rest_1_
  13.7 1.6 %shard_map.141 = (bf16[144,256]{1,0:T(8,128)(2,1)}, bf16[144,256]{1,0:T(8,128)(2,1)}) custom-call(bf16[144,384]{1,0:T(8,128)(2,1)} %copy-done.14, bf16[144,384]{1,0:T(8,128)(2,1)} %copy-done.15), custom_call_target="tpu_custom_call" | custom-call | tf_op jit(solution)/shard_map/pallas_call | solution.py:495
  15.4 1.7 %collective-permute-start.5 = (bf16[144,256]{1,0:T(8,128)(2,1)}, bf16[144,256]{1,0:T(8,128)(2,1)S(1)}, u32[]{:S(2)}, u32[]{:S(2)}) collective-permute-start(bf16[144,256]{1,0:T(8,128)(2,1)} %get-tuple-element.47), channel_id=1, source_target_pairs={{8,0},{16,8},{24,16},{0,24},{9,1},{17,9},{25,17},{1,25},{10,2},{18... | collective-permute-start | bytes 221192 | tf_op jit(solution)/shard_map/ppermute | solution.py:507
  17.1 2.2 %shard_map.142 = (bf16[256,128]{1,0:T(8,128)(2,1)}, bf16[256,128]{1,0:T(8,128)(2,1)}, bf16[256,64]{1,0:T(8,128)(2,1)}, bf16[256,256]{1,0:T(8,128)(2,1)}, bf16[25...) custom-call(bf16[128,256]{1,0:T(8,128)(2,1)} %w_emb_ref.1, ...), custom_call_target="tpu_custom_call" | custom-call | tf_op jit(solution)/shard_map/pallas_call | solution.py:495
  20.2 2.3 %shard_map.143 = (bf16[144,2560]{1,0:T(8,128)(2,1)}, bf16[144,128]{1,0:T(8,128)(2,1)}) custom-call(f32[3,1,512]{2,1,0:T(1,128)} %bitcast.21, bf16[144,512]{1,0:T(8,128)(2,1)} %get-tuple-element.41.own_ref, s32[1,128]{1,0:T(1,128)} %bitcast.25, bf16[144,384]{1,0:T(8,128)(2,1)} %copy-done.14, bf16[144,384]{1,0:T(8,128)(2,1)} %copy-done.15, ...), custom_call_target="tpu_custom_call" | custom-call | tf_op jit(solution)/shard_map/pallas_call | solution.py:495
  22.5 1.5 %collective-permute-start.6 = (bf16[144,128]{1,0:T(8,128)(2,1)}, bf16[144,128]{1,0:T(8,128)(2,1)S(1)}, u32[]{:S(2)}, u32[]{:S(2)}) collective-permute-start(bf16[144,128]{1,0:T(8,128)(2,1)} %get-tuple-element.62), channel_id=1, source_target_pairs={{0,1},{1,0},{2,3},{3,2},{4,5},{5,4},{6,7},{7,6},{8,9},{9,8},{10,11... | collective-permute-start | bytes 110600 | tf_op jit(solution)/shard_map/ppermute | solution.py:512
  24.6 2.9 %shard_map.144 = (bf16[256,2560]{1,0:T(8,128)(2,1)}, f32[6,24,128]{2,1,0:T(8,128)}) custom-call(bf16[144,2560]{1,0:T(8,128)(2,1)} %get-tuple-element.58.inner_ref, bf16[256,128]{1,0:T(8,128)(2,1)} %get-tuple-element.59.w_emb_ref), custom_call_target="tpu_custom_call" | custom-call | tf_op jit(solution)/shard_map/pallas_call | solution.py:495
  27.7 1.3 %copy-done = bf16[256,2560]{1,0:T(8,128)(2,1)S(1)} copy-done((bf16[256,2560]{1,0:T(8,128)(2,1)S(1)}, bf16[256,2560]{1,0:T(8,128)(2,1)}, u32[]{:S(2)}) %copy-start) | copy-done | bytes 1310744
  29.0 0.9 copy-done.7
  29.9 54.8 %shard_map.145 = (f32[3,24,128]{2,1,0:T(8,128)S(1)}, f32[3,128]{1,0:T(4,128)S(1)}, f32[1,512]{1,0:T(1,128)}) custom-call(s32[1]{0:T(128)} %bitcast.14.count_ref, f32[1]{0:T(128)} %bitcast.1.lift_ref, s32[12,1,512]{2,1,0:T(1,128)S(1)} %bitcast.17, s32[12,1,512]{2,1,0:T(1,128)S(1)} %bitcast.18, bf16[256,2560]{1,0:T(8,128)(2,1)S(1)} %copy-done, ...), custom_call_target="tpu_custom_call" | custom-call | tf_op jit(solution)/shard_map/pallas_call | solution.py:495
  85.9 3.0 %collective-permute-done.7.back_ref = f32[3,128]{1,0:T(4,128)S(1)} collective-permute-done((f32[3,128]{1,0:T(4,128)S(1)}, f32[3,128]{1,0:T(4,128)S(1)}, u32[]{:S(2)}, u32[]{:S(2)}) %collective-permute-start.7) | collective-permute-done | bytes 1568 | tf_op jit(solution)/shard_map/ppermute | solution.py:512
  89.4 1.6 %shard_map.146 = (f32[3,8,128]{2,1,0:T(8,128)}, f32[15,128]{1,0:T(8,128)}, f32[15,128]{1,0:T(8,128)}, f32[9,128]{1,0:T(8,128)}, f32[9,128]{1,0:T(8,128)}) custom-call(f32[3,24,128]{2,1,0:T(8,128)} %copy-done.10, f32[3,128]{1,0:T(4,128)} %copy-done.24, s32[1,128]{1,0:T(1,128)} %bitcast.26), custom_call_target="tpu_custom_call" | custom-call | tf_op jit(solution)/shard_map/pallas_call | solution.py:495
  91.5 1.3 %collective-permute-done.8.from_xp_ref = f32[15,128]{1,0:T(8,128)S(1)} collective-permute-done((f32[15,128]{1,0:T(8,128)}, f32[15,128]{1,0:T(8,128)S(1)}, u32[]{:S(2)}, u32[]{:S(2)}) %collective-permute-start.8) | collective-permute-done | bytes 7712 | tf_op jit(solution)/shard_map/ppermute | solution.py:507
  92.9 1.7 %collective-permute-done.9.from_xm_ref = f32[15,128]{1,0:T(8,128)S(1)} collective-permute-done((f32[15,128]{1,0:T(8,128)}, f32[15,128]{1,0:T(8,128)S(1)}, u32[]{:S(2)}, u32[]{:S(2)}) %collective-permute-start.9) | collective-permute-done | bytes 7712 | tf_op jit(solution)/shard_map/ppermute | solution.py:507
  95.2 1.4 %shard_map.147 = (f32[9,128]{1,0:T(8,128)}, f32[9,128]{1,0:T(8,128)}) custom-call(f32[15,128]{1,0:T(8,128)} %copy-done.20, f32[15,128]{1,0:T(8,128)} %copy-done.21, f32[9,128]{1,0:T(8,128)} %get-tuple-element.76.to_ym_ref, f32[9,128]{1,0:T(8,128)} %get-tuple-element.77.to_yp_ref), custom_call_target="tpu_custom_call" | custom-call | tf_op jit(solution)/shard_map/pallas_call | solution.py:495
  96.5 2.9 %collective-permute-start.10 = (f32[9,128]{1,0:T(8,128)}, f32[9,128]{1,0:T(8,128)S(1)}, u32[]{:S(2)}, u32[]{:S(2)}) collective-permute-start(f32[9,128]{1,0:T(8,128)} %get-tuple-element.78), channel_id=1, source_target_pairs={{2,0},{4,2},{6,4},{0,6},{3,1},{5,3},{7,5},{1,7},{10,8},{12,10},{14... | collective-permute-start | bytes 13832 | tf_op jit(solution)/shard_map/ppermute | solution.py:507
  99.5 1.6 %collective-permute-done.10.from_yp_ref = f32[9,128]{1,0:T(8,128)S(1)} collective-permute-done((f32[9,128]{1,0:T(8,128)}, f32[9,128]{1,0:T(8,128)S(1)}, u32[]{:S(2)}, u32[]{:S(2)}) %collective-permute-start.10) | collective-permute-done | bytes 4640 | tf_op jit(solution)/shard_map/ppermute | solution.py:507
  101.0 4.1 %collective-permute-done.11.from_ym_ref = f32[9,128]{1,0:T(8,128)S(1)} collective-permute-done((f32[9,128]{1,0:T(8,128)}, f32[9,128]{1,0:T(8,128)S(1)}, u32[]{:S(2)}, u32[]{:S(2)}) %collective-permute-start.11) | collective-permute-done | bytes 4640 | tf_op jit(solution)/shard_map/ppermute | solution.py:507
  105.7 1.7 %shard_map.148 = f32[3,1,512]{2,1,0:T(1,128)} custom-call(f32[3,8,128]{2,1,0:T(8,128)} %get-tuple-element.73.own_ref, s32[8,128]{1,0:T(8,128)} %bitcast.23, f32[15,128]{1,0:T(8,128)} %copy-done.20, f32[15,128]{1,0:T(8,128)} %copy-done.21, f32[9,128]{1,0:T(8,128)} %copy-done.22, f32[9,128]{1,0:T(8,128)} %copy-done.23), custom_call_target="tpu_custom_call" | custom-call | tf_op jit(solution)/shard_map/pallas_call | solution.py:495
  (59 shorter events, 4.9 us)
Async XLA Ops:
  0.6 26.9 %copy-start.3 = (bf16[256,64]{0,1:T(8,128)(2,1)S(1)}, bf16[256,64]{0,1:T(8,128)(2,1)}, u32[]{:S(2)}) copy-start(bf16[256,64]{0,1:T(8,128)(2,1)} %param.22) | copy-start | bytes 98308
  0.6 26.9 %copy-start.11 = (s32[1,1,1,6144]{3,2,1,0:T(1,128)S(1)}, s32[1,1,1,6144]{3,2,1,0:T(1,128)}, u32[]{:S(2)}) copy-start(s32[1,1,1,6144]{3,2,1,0:T(1,128)} %param.15) | copy-start | bytes 73732
  0.7 26.9 %copy-start.12 = (s32[1,1,1,6144]{3,2,1,0:T(1,128)S(1)}, s32[1,1,1,6144]{3,2,1,0:T(1,128)}, u32[]{:S(2)}) copy-start(s32[1,1,1,6144]{3,2,1,0:T(1,128)} %param.16) | copy-start | bytes 73732
  3.0 9.1 %collective-permute-start = (bf16[144,384]{1,0:T(8,128)(2,1)}, bf16[144,384]{1,0:T(8,128)(2,1)S(1)}, u32[]{:S(2)}, u32[]{:S(2)}) collective-permute-start(bf16[144,384]{1,0:T(8,128)(2,1)} %get-tuple-element.42), channel_id=1, source_target_pairs={{6,0},{0,2},{2,4},{4,6},{7,1},{1,3},{3,5},{5,7},{14,8},{8,10},{10,... | collective-permute-start | bytes 331784 | tf_op jit(solution)/shard_map/ppermute | solution.py:507
  6.0 7.1 %collective-permute-start.1 = (bf16[144,384]{1,0:T(8,128)(2,1)}, bf16[144,384]{1,0:T(8,128)(2,1)S(1)}, u32[]{:S(2)}, u32[]{:S(2)}) collective-permute-start(bf16[144,384]{1,0:T(8,128)(2,1)} %get-tuple-element.43), channel_id=1, source_target_pairs={{2,0},{4,2},{6,4},{0,6},{3,1},{5,3},{7,5},{1,7},{10,8},{12,10},{14... | collective-permute-start | bytes 331784 | tf_op jit(solution)/shard_map/ppermute | solution.py:507
  8.0 11.4 %collective-permute-start.2 = (bf16[144,384]{1,0:T(8,128)(2,1)}, bf16[144,384]{1,0:T(8,128)(2,1)S(1)}, u32[]{:S(2)}, u32[]{:S(2)}) collective-permute-start(bf16[144,384]{1,0:T(8,128)(2,1)} %get-tuple-element.44), channel_id=1, source_target_pairs={{24,0},{0,8},{8,16},{16,24},{25,1},{1,9},{9,17},{17,25},{26,2},{2,... | collective-permute-start | bytes 331784 | tf_op jit(solution)/shard_map/ppermute | solution.py:507
  8.0 11.4 %collective-permute-start.3 = (bf16[144,384]{1,0:T(8,128)(2,1)}, bf16[144,384]{1,0:T(8,128)(2,1)S(1)}, u32[]{:S(2)}, u32[]{:S(2)}) collective-permute-start(bf16[144,384]{1,0:T(8,128)(2,1)} %get-tuple-element.45), channel_id=1, source_target_pairs={{8,0},{16,8},{24,16},{0,24},{9,1},{17,9},{25,17},{1,25},{10,2},{18... | collective-permute-start | bytes 331784 | tf_op jit(solution)/shard_map/ppermute | solution.py:507
  15.4 4.0 %collective-permute-start.4 = (bf16[144,256]{1,0:T(8,128)(2,1)}, bf16[144,256]{1,0:T(8,128)(2,1)S(1)}, u32[]{:S(2)}, u32[]{:S(2)}) collective-permute-start(bf16[144,256]{1,0:T(8,128)(2,1)} %get-tuple-element.46), channel_id=1, source_target_pairs={{24,0},{0,8},{8,16},{16,24},{25,1},{1,9},{9,17},{17,25},{26,2},{2,... | collective-permute-start | bytes 221192 | tf_op jit(solution)/shard_map/ppermute | solution.py:507
  15.4 4.0 %collective-permute-start.5 = (bf16[144,256]{1,0:T(8,128)(2,1)}, bf16[144,256]{1,0:T(8,128)(2,1)S(1)}, u32[]{:S(2)}, u32[]{:S(2)}) collective-permute-start(bf16[144,256]{1,0:T(8,128)(2,1)} %get-tuple-element.47), channel_id=1, source_target_pairs={{8,0},{16,8},{24,16},{0,24},{9,1},{17,9},{25,17},{1,25},{10,2},{18... | collective-permute-start | bytes 221192 | tf_op jit(solution)/shard_map/ppermute | solution.py:507
  19.3 8.2 %copy-start.1 = (bf16[256,128]{1,0:T(8,128)(2,1)S(1)}, bf16[256,128]{1,0:T(8,128)(2,1)}, u32[]{:S(2)}) copy-start(bf16[256,128]{1,0:T(8,128)(2,1)} %get-tuple-element.59.w_emb_ref) | copy-start | bytes 196612
  19.3 8.2 %copy-start.2 = (bf16[448,256]{1,0:T(8,128)(2,1)S(1)}, bf16[448,256]{1,0:T(8,128)(2,1)}, u32[]{:S(2)}) copy-start(bf16[448,256]{1,0:T(8,128)(2,1)} %get-tuple-element.67.w_back_ref) | copy-start | bytes 688132
  19.3 8.2 %copy-start.4 = (bf16[256,256]{1,0:T(8,128)(2,1)S(1)}, bf16[256,256]{1,0:T(8,128)(2,1)}, u32[]{:S(2)}) copy-start(bf16[256,256]{1,0:T(8,128)(2,1)} %get-tuple-element.65.w_lat_t_ref) | copy-start | bytes 393220
  19.4 8.2 %copy-start.5 = (bf16[256,192]{1,0:T(8,128)(2,1)S(1)}, bf16[256,192]{1,0:T(8,128)(2,1)}, u32[]{:S(2)}) copy-start(bf16[256,192]{1,0:T(8,128)(2,1)} %get-tuple-element.66.w_ten_t_ref) | copy-start | bytes 294916
  19.4 8.2 %copy-start.6 = (f32[256,128]{1,0:T(8,128)S(1)}, f32[256,128]{1,0:T(8,128)}, u32[]{:S(2)}) copy-start(f32[256,128]{1,0:T(8,128)} %get-tuple-element.68.w_out_ref) | copy-start | bytes 393220
  19.4 8.2 %copy-start.8 = (bf16[256,128]{1,0:T(8,128)(2,1)S(1)}, bf16[256,128]{1,0:T(8,128)(2,1)}, u32[]{:S(2)}) copy-start(bf16[256,128]{1,0:T(8,128)(2,1)} %get-tuple-element.63.w_rad_ref) | copy-start | bytes 196612
  19.4 8.2 %copy-start.9 = (bf16[256,64]{1,0:T(8,128)(2,1)S(1)}, bf16[256,64]{1,0:T(8,128)(2,1)}, u32[]{:S(2)}) copy-start(bf16[256,64]{1,0:T(8,128)(2,1)} %get-tuple-element.64.w_chan_ref) | copy-start | bytes 98308
  19.4 8.2 %copy-start.13 = (bf16[16,256]{1,0:T(8,128)(2,1)S(1)}, bf16[16,256]{1,0:T(8,128)(2,1)}, u32[]{:S(2)}) copy-start(bf16[16,256]{1,0:T(8,128)(2,1)} %get-tuple-element.69.w_rbf_ref) | copy-start | bytes 24580
  22.5 5.0 %collective-permute-start.6 = (bf16[144,128]{1,0:T(8,128)(2,1)}, bf16[144,128]{1,0:T(8,128)(2,1)S(1)}, u32[]{:S(2)}, u32[]{:S(2)}) collective-permute-start(bf16[144,128]{1,0:T(8,128)(2,1)} %get-tuple-element.62), channel_id=1, source_target_pairs={{0,1},{1,0},{2,3},{3,2},{4,5},{5,4},{6,7},{7,6},{8,9},{9,8},{10,11... | collective-permute-start | bytes 110600 | tf_op jit(solution)/shard_map/ppermute | solution.py:512
  85.3 3.6 %collective-permute-start.7 = (f32[3,128]{1,0:T(4,128)S(1)}, f32[3,128]{1,0:T(4,128)S(1)}, u32[]{:S(2)}, u32[]{:S(2)}) collective-permute-start(f32[3,128]{1,0:T(4,128)S(1)} %get-tuple-element.72), channel_id=1, source_target_pairs={{0,1},{1,0},{2,3},{3,2},{4,5},{5,4},{6,7},{7,6},{8,9},{9,8},{10,11... | collective-permute-start | bytes 4616 | tf_op jit(solution)/shard_map/ppermute | solution.py:512
  91.0 1.8 %collective-permute-start.8 = (f32[15,128]{1,0:T(8,128)}, f32[15,128]{1,0:T(8,128)S(1)}, u32[]{:S(2)}, u32[]{:S(2)}) collective-permute-start(f32[15,128]{1,0:T(8,128)} %get-tuple-element.74), channel_id=1, source_target_pairs={{8,0},{16,8},{24,16},{0,24},{9,1},{17,9},{25,17},{1,25},{10,2},{18... | collective-permute-start | bytes 23048 | tf_op jit(solution)/shard_map/ppermute | solution.py:507
  91.3 3.3 %collective-permute-start.9 = (f32[15,128]{1,0:T(8,128)}, f32[15,128]{1,0:T(8,128)S(1)}, u32[]{:S(2)}, u32[]{:S(2)}) collective-permute-start(f32[15,128]{1,0:T(8,128)} %get-tuple-element.75), channel_id=1, source_target_pairs={{24,0},{0,8},{8,16},{16,24},{25,1},{1,9},{9,17},{17,25},{26,2},{2,... | collective-permute-start | bytes 23048 | tf_op jit(solution)/shard_map/ppermute | solution.py:507
  96.5 4.5 %collective-permute-start.10 = (f32[9,128]{1,0:T(8,128)}, f32[9,128]{1,0:T(8,128)S(1)}, u32[]{:S(2)}, u32[]{:S(2)}) collective-permute-start(f32[9,128]{1,0:T(8,128)} %get-tuple-element.78), channel_id=1, source_target_pairs={{2,0},{4,2},{6,4},{0,6},{3,1},{5,3},{7,5},{1,7},{10,8},{12,10},{14... | collective-permute-start | bytes 13832 | tf_op jit(solution)/shard_map/ppermute | solution.py:507
  99.4 5.7 %collective-permute-start.11 = (f32[9,128]{1,0:T(8,128)}, f32[9,128]{1,0:T(8,128)S(1)}, u32[]{:S(2)}, u32[]{:S(2)}) collective-permute-start(f32[9,128]{1,0:T(8,128)} %get-tuple-element.79), channel_id=1, source_target_pairs={{6,0},{0,2},{2,4},{4,6},{7,1},{1,3},{3,5},{5,7},{14,8},{8,10},{10,... | collective-permute-start | bytes 13832 | tf_op jit(solution)/shard_map/ppermute | solution.py:507
  101.0 4.1 %copy-start.22 = (f32[9,128]{1,0:T(8,128)}, f32[9,128]{1,0:T(8,128)S(1)}, u32[]{:S(2)}) copy-start(f32[9,128]{1,0:T(8,128)S(1)} %collective-permute-done.10.from_yp_ref) | copy-start | bytes 13828
  (13 other events, 10.6 us)

commit v3 on v2

--- a/solution.py
+++ b/solution.py
@@ -9,6 +9,7 @@
 bf16 = jnp.bfloat16
 LANES = 128
 PARTS = 16
+BLOCK = 256
 ROOT3 = 3.0**0.5
 BANDS = (0, 1, 1, 1, 2, 2, 2, 2, 2)
 
@@ -58,8 +59,9 @@
     return (hot_low.reshape(size // 16, 16, lanes) * mask[None]).reshape(size, lanes)
 
 
-def sigmoid(x):
-    return 0.5 * jnp.tanh(0.5 * x) + 0.5
+def half_silu(x):
+    half = 0.5 * x
+    return (0.5 * (half * (1.0 + jnp.tanh(half)))).astype(bf16)
 
 
 def pack_kernel(pos_ref, attr_ref, rim_ref, own_ref, *rest):
@@ -151,13 +153,13 @@
     eye_b = eye.astype(bf16)
     emb_t_ref[...] = dot_t(eye_b, w_emb_ref[...]).astype(bf16)
     chan_ref[...] = dot_t(eye_b, w_chan_t_ref[...]).astype(bf16)
-    lat_t_ref[...] = dot_t(eye_b, w_lat_ref[...]).astype(bf16)
-    ten_t_ref[...] = dot_t(eye_b, w_ten_ref[...]).astype(bf16)
+    lat_t_ref[...] = (0.5 * dot_t(eye_b, w_lat_ref[...])).astype(bf16)
+    ten_t_ref[...] = (0.5 * dot_t(eye_b, w_ten_ref[...])).astype(bf16)
     back_ref[0:features, :] = w_lat_ref[...]
     back_ref[features:, :] = w_ten_ref[...]
     column = jnp.sum(eye * w_out_ref[...], axis=1, keepdims=True)
     out_ref[...] = jnp.broadcast_to(column, out_ref.shape)
-    upper, lower = halves(w_rbf_ref[...])
+    upper, lower = halves(0.5 * w_rbf_ref[...])
     rbf_ref[...] = jnp.concatenate([upper, lower], axis=0).astype(bf16)
     scratch[...] = jnp.zeros_like(scratch)
     for start, value in ((0, upper), (8, upper), (16, lower), (24, lower)):
@@ -170,11 +172,66 @@
     inner_len = inner_ref.shape[1]
     for first in range(0, inner_len, 512):
         raw = dot(w_emb_ref[...], inner_ref[0:width, first : first + 512])
-        feat_ref[:, first : first + 512] = (raw * sigmoid(raw)).astype(bf16)
+        feat_ref[:, first : first + 512] = half_silu(raw)
     parts = inner_ref[width:, :].astype(f32)
     place_ref[...] = jnp.zeros_like(place_ref)
     for high in range(inner_len // LANES):
         place_ref[0:6, high, :] = parts[0:6, high * LANES : (high + 1) * LANES]
+
+
+def bucket_kernel(count_ref, centers_ref, others_ref, center_ref, other_ref, meta_ref, rows_s, low_s):
+    lines = centers_ref.shape[0]
+    count = count_ref[0]
+    c, o = centers_ref[...], others_ref[...]
+    shape = (lines, LANES)
+    order = rows_of(shape) * LANES + lax.broadcasted_iota(jnp.int32, shape, 1)
+    half = lax.shift_right_logical(c, 8)
+    marks = [
+        jnp.where(order < count, jnp.where(half == h, 1.0, 0.0), 0.0) for h in range(2)
+    ]
+    square = (LANES, LANES)
+    tri = jnp.where(rows_of(square) < lax.broadcasted_iota(jnp.int32, square, 1), 1.0, 0.0)
+    tall = (lines, lines)
+    below = jnp.where(lax.broadcasted_iota(jnp.int32, tall, 1) < rows_of(tall), 1.0, 0.0)
+    starts = [0.0, None]
+    slot = jnp.full(shape, -1.0, f32)
+    for h in range(2):
+        mark = marks[h].astype(bf16)
+        inside = dot(mark, tri.astype(bf16))
+        totals = dot(mark, jnp.ones(square, bf16))
+        before = dot(below.astype(bf16), totals.astype(bf16))
+        everything = jnp.sum(totals, axis=0, keepdims=True)
+        if h == 0:
+            blocks = jnp.floor((everything + (BLOCK - 1)) * (1.0 / BLOCK))
+            starts[1] = blocks * BLOCK
+            first_blocks = blocks
+        else:
+            blocks = first_blocks + jnp.floor((everything + (BLOCK - 1)) * (1.0 / BLOCK))
+        slot = jnp.where(marks[h] > 0.0, starts[h] + before + inside, slot)
+    meta_ref[0:1, :] = first_blocks.astype(jnp.int32)
+    meta_ref[1:2, :] = blocks.astype(jnp.int32)
+    slot = slot.astype(jnp.int32)
+    slot_high = lax.shift_right_arithmetic(slot, 7)
+    slot_low = lax.bitwise_and(slot, LANES - 1)
+    highs = center_ref.shape[0]
+    values = [
+        jnp.ones(shape, f32),
+        lax.bitwise_and(c, 255).astype(f32),
+        lax.shift_right_logical(o, 7).astype(f32),
+        lax.bitwise_and(o, LANES - 1).astype(f32),
+    ]
+    for line in range(lines):
+        lanes = slice(line * LANES, (line + 1) * LANES)
+        high = one_hot(slot_high[line : line + 1], highs)
+        rows_s[:, lanes] = jnp.concatenate(
+            [high * value[line : line + 1] for value in values], axis=0
+        ).astype(bf16)
+        low_s[:, lanes] = one_hot(slot_low[line : line + 1], LANES).astype(bf16)
+    placed = dot_t(rows_s[...], low_s[...])
+    center = placed[highs : 2 * highs] + placed[0:highs] - 1.0
+    other = placed[2 * highs : 3 * highs] * float(LANES) + placed[3 * highs :]
+    center_ref[...] = center.astype(jnp.int32)
+    other_ref[...] = other.astype(jnp.int32)
 
 
 def harmonic_rows(x, y, z):
@@ -196,7 +253,7 @@
 
 
 def edge_kernel(
-    count_ref,
+    meta_ref,
     lift_ref,
     centers_ref,
     others_ref,
@@ -217,10 +274,12 @@
     energy_ref,
     feat,
     place,
-    hot,
+    place_b,
+    own_b,
+    hot_a,
+    hot_b,
     center_hot,
     low_o,
-    low_c,
     latent_s,
     slope_s,
     chan_s,
@@ -229,25 +288,25 @@
     dharm_s,
     tensor,
     tensor_b,
-    dtensor,
     acc_o,
     acc_c,
 ):
-    blocks, _, eb = centers_ref.shape
+    eb = centers_ref.shape[2]
     width = w_emb_ref.shape[1]
     features = feat_in_ref.shape[0]
     inner_len = feat_in_ref.shape[1]
     table = inner_len + LANES
     highs = table // LANES
-    atoms = tensor.shape[1]
-    c_highs = atoms // LANES
+    span = tensor.shape[2]
+    halves_n = tensor.shape[0]
     chans = w_chan_t_ref.shape[0]
     hpad = place_in_ref.shape[1]
-    count = count_ref[0]
+    first_blocks = meta_ref[0, 0]
+    pairs = (meta_ref[1, 0] + 1) // 2
 
     feat[:, 0:inner_len] = feat_in_ref[...]
     raw = dot(w_emb_ref[...], slab_ref[0:width, :])
-    feat[:, inner_len:table] = (raw * sigmoid(raw)).astype(bf16)
+    feat[:, inner_len:table] = half_silu(raw)
     feat[:, table : table + LANES] = w_rad_ref[...]
     place[...] = place_in_ref[...]
     arrived = slab_ref[width:, :].astype(f32)
@@ -256,35 +315,46 @@
     upper, lower = halves(joined)
     place[0:3, highs - 1, :] = upper
     place[3:6, highs - 1, :] = lower
-    hot[table:, :] = jnp.zeros((hot.shape[0] - table, eb), bf16)
+    place_b[...] = place[...].reshape(6 * hpad, LANES).astype(bf16)
+    own_b[...] = place[:, 0:8, :].reshape(48, LANES).astype(bf16)
+    for hot in (hot_a, hot_b):
+        hot[table:, :] = jnp.zeros((hot.shape[0] - table, eb), bf16)
     tensor[...] = jnp.zeros_like(tensor)
-    dtensor[...] = jnp.zeros_like(dtensor)
     acc_o[...] = jnp.zeros_like(acc_o)
     acc_c[...] = jnp.zeros_like(acc_c)
 
-    def first_pass(b, carry):
-        c = centers_ref[b]
+    def half_of(b):
+        return jnp.where(b >= first_blocks, 1, 0)
+
+    def prepare(b, hot):
+        slot_c = centers_ref[b]
         o = others_ref[b]
-        live = jnp.where(
-            lax.broadcasted_iota(jnp.int32, (1, eb), 1) + b * eb < count, 1.0, 0.0
-        )
+        live = jnp.where(slot_c >= 0, 1.0, 0.0)
+        c = jnp.maximum(slot_c, 0)
+        half = half_of(b)
         c_high = lax.shift_right_logical(c, 7)
         o_high = lax.shift_right_logical(o, 7)
         hot_c = one_hot(lax.bitwise_and(c, LANES - 1), LANES).astype(bf16)
         hot_o = one_hot(lax.bitwise_and(o, LANES - 1), LANES).astype(bf16)
-        low_c[b] = hot_c
         low_o[b] = hot_o
         c_high16 = jnp.broadcast_to(c_high, (16, eb))
         o_high16 = jnp.broadcast_to(o_high, (16, eb))
-
-        place_rows = place[...].reshape(6 * hpad, LANES).astype(bf16)
-        picked = dot(place_rows, hot_o)
+        for high in range(highs):
+            hot[high * LANES : (high + 1) * LANES, :] = masked(hot_o, o_high16, high)
+        own = jnp.concatenate(
+            [masked(hot_c, c_high16, high) for high in range(span // LANES)], axis=0
+        )
+        center_hot[b] = own
+        rows = pl.ds(pl.multiple_of(half * span, span), span)
+        hot[rows, :] += own
+
+        picked = dot(place_b[...], hot_o)
         picked = (picked[0 : 3 * hpad] + picked[3 * hpad :]).reshape(3, hpad, eb)
         po = jnp.sum(picked * one_hot(o_high, hpad)[None], axis=1)
-        own_rows = place[:, 0:8, :].reshape(48, LANES).astype(bf16)
-        picked = dot(own_rows, hot_c)
+        picked = dot(own_b[...], hot_c)
         picked = (picked[0:24] + picked[24:48]).reshape(3, 8, eb)
-        pc = jnp.sum(picked * one_hot(c_high, 8)[None], axis=1)
+        c_whole = c_high + half * (span // LANES)
+        pc = jnp.sum(picked * one_hot(c_whole, 8)[None], axis=1)
         sep = po - pc
         rx, ry, rz = sep[0:1], sep[1:2], sep[2:3]
         squared = rx * rx + ry * ry + rz * rz
@@ -300,80 +370,107 @@
         radial = jnp.concatenate([upper, lower], axis=0).astype(bf16)
         hot[table : table + 16, :] = radial
         hot[table + 16 : table + 32, :] = radial
-
-        for high in range(highs):
-            chunk = masked(hot_o, o_high16, high)
-            if high < c_highs:
-                own = masked(hot_c, c_high16, high)
-                center_hot[b, high * LANES : (high + 1) * LANES, :] = own
-                chunk = chunk + own
-            hot[high * LANES : (high + 1) * LANES, :] = chunk
-
-        mixed = dot(feat[...], hot[...])
-        s = sigmoid(mixed)
-        value = mixed * s
+        return x, y, z, live
+
+    def activate(b, mixed):
+        up = 1.0 + jnp.tanh(mixed)
+        value = mixed * up
         latent = value.astype(bf16)
         latent_s[b] = latent
-        slope_s[b] = (s + value * (1.0 - s)).astype(bf16)
+        slope_s[b] = (up + value * (2.0 - up)).astype(bf16)
+        return latent
+
+    def spread(b, latent, geo):
+        x, y, z, live = geo
         chan = dot(w_chan_t_ref[...], latent) * live
         chan_s[b] = chan
-        harm = harmonic_rows(x, y, z)
-        products = jnp.concatenate(
-            [(chan if h is None else chan * h).astype(bf16) for h in harm], axis=0
+        return jnp.concatenate(
+            [
+                (chan if h is None else chan * h).astype(bf16)
+                for h in harmonic_rows(x, y, z)
+            ],
+            axis=0,
         )
-        tensor[...] += dot_t(products, center_hot[b])
+
+    def first_pass(pair, carry):
+        a, b = 2 * pair, 2 * pair + 1
+        geo_a = prepare(a, hot_a)
+        mixed_a = dot(feat[...], hot_a[...])
+        geo_b = prepare(b, hot_b)
+        mixed_b = dot(feat[...], hot_b[...])
+        latent_a = activate(a, mixed_a)
+        products_a = spread(a, latent_a, geo_a)
+        latent_b = activate(b, mixed_b)
+        tensor[half_of(a)] += dot_t(products_a, center_hot[a])
+        products_b = spread(b, latent_b, geo_b)
+        tensor[half_of(b)] += dot_t(products_b, center_hot[b])
         return carry
 
-    lax.fori_loop(0, blocks, first_pass, 0)
+    lax.fori_loop(0, pairs, first_pass, 0)
     tensor_b[...] = (0.125 * tensor[...]).astype(bf16)
-
-    def second_pass(b, carry):
+    tensor[...] = jnp.zeros_like(tensor)
+
+    def invariants(b, gathered):
         geo = geo_s[b]
-        x, y, z = geo[0:1], geo[1:2], geo[2:3]
-        env, live = geo[5:6], geo[7:8]
-        harm = harmonic_rows(x, y, z)
-        gathered = dot(tensor_b[...], center_hot[b])
+        harm = harmonic_rows(geo[0:1], geo[1:2], geo[2:3])
         parts = [gathered[m * chans : (m + 1) * chans] for m in range(9)]
         bands = [parts[0], None, None]
         for m in range(1, 9):
             term = parts[m] * harm[m]
             band = BANDS[m]
             bands[band] = term if bands[band] is None else bands[band] + term
-        invariant = jnp.concatenate([band.astype(bf16) for band in bands], axis=0)
-        pre = dot(w_lat_t_ref[...], latent_s[b]) + dot(w_ten_t_ref[...], invariant)
-        s = sigmoid(pre)
-        value = pre * s
+        return jnp.concatenate([band.astype(bf16) for band in bands], axis=0)
+
+    def hidden(b, invariant):
+        return dot(w_lat_t_ref[...], latent_s[b]) + dot(w_ten_t_ref[...], invariant)
+
+    def readout(b, pre):
+        geo = geo_s[b]
+        up = 1.0 + jnp.tanh(pre)
+        value = pre * up
         weight = jnp.concatenate([w_out_ref[...]] * (eb // LANES), axis=1)
-        summed = jnp.sum(value * weight, axis=0, keepdims=True)
-        geo_s[b, 8:9, :] = summed
-        dpre = (weight * (env * live) * (s + value * (1.0 - s))).astype(bf16)
-        back = dot(w_back_ref[...], dpre)
+        geo_s[b, 8:9, :] = jnp.sum(value * weight, axis=0, keepdims=True)
+        scale = 0.5 * geo[5:6] * geo[7:8]
+        return ((up + value * (2.0 - up)) * (weight * scale)).astype(bf16)
+
+    def unfold(b, back, gathered):
+        geo = geo_s[b]
+        harm = harmonic_rows(geo[0:1], geo[1:2], geo[2:3])
         dlat_s[b] = back[0:features].astype(bf16)
         dbands = [
             back[features + band * chans : features + (band + 1) * chans] for band in range(3)
         ]
-        products = jnp.concatenate(
+        for m in range(1, 9):
+            part = gathered[m * chans : (m + 1) * chans]
+            dharm_s[b, (m - 1) * 8 : m * 8, :] = fold8(dbands[BANDS[m]] * part)
+        return jnp.concatenate(
             [
                 (dbands[BANDS[m]] if harm[m] is None else dbands[BANDS[m]] * harm[m]).astype(bf16)
                 for m in range(9)
             ],
             axis=0,
         )
-        dtensor[...] += dot_t(products, center_hot[b])
-        for m in range(1, 9):
-            dharm_s[b, (m - 1) * 8 : m * 8, :] = fold8(dbands[BANDS[m]] * parts[m])
+
+    def second_pass(pair, carry):
+        a, b = 2 * pair, 2 * pair + 1
+        gathered_a = dot(tensor_b[half_of(a)], center_hot[a])
+        gathered_b = dot(tensor_b[half_of(b)], center_hot[b])
+        pre_a = hidden(a, invariants(a, gathered_a))
+        pre_b = hidden(b, invariants(b, gathered_b))
+        back_a = dot(w_back_ref[...], readout(a, pre_a))
+        back_b = dot(w_back_ref[...], readout(b, pre_b))
+        products_a = unfold(a, back_a, gathered_a)
+        tensor[half_of(a)] += dot_t(products_a, center_hot[a])
+        products_b = unfold(b, back_b, gathered_b)
+        tensor[half_of(b)] += dot_t(products_b, center_hot[b])
         return carry
 
-    lax.fori_loop(0, blocks, second_pass, 0)
-    tensor_b[...] = (0.125 * dtensor[...]).astype(bf16)
-
-    def third_pass(b, carry):
+    lax.fori_loop(0, pairs, second_pass, 0)
+    tensor_b[...] = (0.125 * tensor[...]).astype(bf16)
+
+    def channels_back(b, gathered):
         geo = geo_s[b]
-        x, y, z = geo[0:1], geo[1:2], geo[2:3]
-        inv_d, dist, env, squared = geo[3:4], geo[4:5], geo[5:6], geo[6:7]
-        live, summed = geo[7:8], geo[8:9]
-        harm = harmonic_rows(x, y, z)
-        gathered = dot(tensor_b[...], center_hot[b])
+        harm = harmonic_rows(geo[0:1], geo[1:2], geo[2:3])
         chan = chan_s[b]
         dchan = gathered[0:chans]
         dh = [None]
@@ -382,11 +479,18 @@
             dchan = dchan + part * harm[m]
             total = dharm_s[b, (m - 1) * 8 : m * 8, :] + fold8(part * chan)
             dh.append(jnp.sum(total, axis=0, keepdims=True))
-        dchan = (dchan * live).astype(bf16)
-        dlat = dlat_s[b].astype(f32) + dot(w_chan_ref[...], dchan)
-        dmixed = (dlat * slope_s[b].astype(f32)).astype(bf16)
-        drad = dot(w_rbf_ref[...], dmixed)
-        drad = drad[0:8] + drad[8:16]
+        return (dchan * geo[7:8]).astype(bf16), dh
+
+    def radial_back(b, dchan):
+        dlat = dlat_s[b] + dot(w_chan_ref[...], dchan).astype(bf16)
+        drad = dot(w_rbf_ref[...], dlat * slope_s[b])
+        return drad[0:8] + drad[8:16]
+
+    def finish(b, drad, dh):
+        geo = geo_s[b]
+        x, y, z = geo[0:1], geo[1:2], geo[2:3]
+        inv_d, dist, env, squared = geo[3:4], geo[4:5], geo[5:6], geo[6:7]
+        live, summed = geo[7:8], geo[8:9]
         mu = 0.5 + 0.4 * rows_of((8, eb)).astype(f32)
         u = (dist - mu) * 2.0
         weighted = drad * jnp.exp(-(u * u))
@@ -401,32 +505,48 @@
         gs = [dx * inv_d + both * x, dy * inv_d + both * y, dz * inv_d + both * z]
         energy = summed * env * live
 
-        c_high = lax.shift_right_logical(centers_ref[b], 7)
         o_high = lax.shift_right_logical(others_ref[b], 7)
         mask_o = one_hot(o_high, hpad)
-        mask_c = one_hot(c_high, 8)
         split = [halves(g) for g in gs]
         rows_o = jnp.concatenate(
             [mask_o * split[d][part] for part in range(2) for d in range(3)], axis=0
         ).astype(bf16)
         split.append(halves(energy))
         rows_c = jnp.concatenate(
-            [mask_c * split[d][part] for part in range(2) for d in range(4)], axis=0
+            [split[d][part] for part in range(2) for d in range(4)]
+            + [jnp.zeros((8, eb), f32)],
+            axis=0,
         ).astype(bf16)
         acc_o[...] += dot_t(rows_o, low_o[b])
-        acc_c[...] += dot_t(rows_c, low_c[b])
+        acc_c[half_of(b)] += dot_t(rows_c, center_hot[b])
+
+    def third_pass(pair, carry):
+        a, b = 2 * pair, 2 * pair + 1
+        gathered_a = dot(tensor_b[half_of(a)], center_hot[a])
+        gathered_b = dot(tensor_b[half_of(b)], center_hot[b])
+        dchan_a, dh_a = channels_back(a, gathered_a)
+        drad_a = radial_back(a, dchan_a)
+        dchan_b, dh_b = channels_back(b, gathered_b)
+        drad_b = radial_back(b, dchan_b)
+        finish(a, drad_a, dh_a)
+        finish(b, drad_b, dh_b)
         return carry
 
-    lax.fori_loop(0, blocks, third_pass, 0)
+    lax.fori_loop(0, pairs, third_pass, 0)
     sum_o = acc_o[0 : 3 * hpad, :] + acc_o[3 * hpad :, :]
-    sum_c = acc_c[0:32, :] + acc_c[32:64, :]
     for d in range(3):
         grad_ref[d] = sum_o[d * hpad : (d + 1) * hpad]
-        grad_ref[d, 0:8, :] = sum_o[d * hpad : d * hpad + 8] - sum_c[d * 8 : (d + 1) * 8]
         slab_grad_ref[d : d + 1, :] = sum_o[d * hpad + highs - 1 : d * hpad + highs]
-    for high in range(c_highs):
-        lanes = slice(high * LANES, (high + 1) * LANES)
-        energy_ref[:, lanes] = sum_c[24 + high : 25 + high]
+    for half in range(halves_n):
+        sum_c = acc_c[half, 0:4, :] + acc_c[half, 4:8, :]
+        for part in range(span // LANES):
+            high = half * (span // LANES) + part
+            lanes = slice(part * LANES, (part + 1) * LANES)
+            for d in range(3):
+                grad_ref[d, high : high + 1, :] = (
+                    sum_o[d * hpad + high : d * hpad + high + 1] - sum_c[d : d + 1, lanes]
+                )
+            energy_ref[:, high * LANES : (high + 1) * LANES] = sum_c[3:4, lanes]
 
 
 def return_kernel(grad_ref, back_ref, zrows_ref, own_ref, to_xm_ref, to_xp_ref, to_ym_ref, to_yp_ref):
@@ -540,12 +660,12 @@
     inner_len = atoms + 16 * LANES
     table = inner_len + LANES
     hpad = -(-(table // LANES) // 8) * 8
-    eb = 512 if edges % 512 == 0 else LANES
-    blocks = edges // eb
-    centers = edge_center.reshape(blocks, 1, eb)
-    others = edge_other.reshape(blocks, 1, eb)
+    eb = BLOCK
+    span = 2 * LANES
+    blocks = -(-(edges // eb + atoms // span - 1) // 2) * 2
+    slot_rows = -(-(blocks * eb // LANES) // 8) * 8
     lift = (1 - 2 * lax.axis_index("gz")).astype(f32).reshape(1)
-    big = 44 * 1024 * 1024
+    big = 36 * 1024 * 1024
 
     shape = jax.ShapeDtypeStruct
     w_chan_t = w_chan.T
@@ -573,6 +693,24 @@
     got = [
         shifted(x, "gx" if way[0] else "gy", way[0] + way[1]) for x, way in zip(sent, sides)
     ]
+    lines = edges // LANES
+    bucketed = call(
+        bucket_kernel,
+        (
+            shape((slot_rows, LANES), jnp.int32),
+            shape((slot_rows, LANES), jnp.int32),
+            shape((2, LANES), jnp.int32),
+        ),
+        (count, edge_center.reshape(lines, LANES), edge_other.reshape(lines, LANES)),
+        [pltpu.VMEM((4 * slot_rows, edges), bf16), pltpu.VMEM((LANES, edges), bf16)],
+        smem=1,
+        limit=24 * 1024 * 1024,
+    )
+    first, bucketed = lax.optimization_barrier((got[:2], bucketed))
+    got = [*first, *got[2:]]
+    centers, others, meta = bucketed
+    centers = centers.reshape(-1, 1, eb)
+    others = others.reshape(-1, 1, eb)
     to_plus, to_minus = call(
         corner_kernel,
         (shape((height, 2 * LANES), bf16),) * 2,
@@ -597,7 +735,7 @@
         edge_kernel,
         (shape((3, hpad, LANES), f32), shape((3, LANES), f32), shape((1, atoms), f32)),
         (
-            count,
+            meta,
             lift,
             centers,
             others,
@@ -617,9 +755,11 @@
         [
             pltpu.VMEM((features, table + LANES), bf16),
             pltpu.VMEM((6, hpad, LANES), f32),
+            pltpu.VMEM((6 * hpad, LANES), bf16),
+            pltpu.VMEM((48, LANES), bf16),
             pltpu.VMEM((table + LANES, eb), bf16),
-            pltpu.VMEM((blocks, atoms, eb), bf16),
-            pltpu.VMEM((blocks, LANES, eb), bf16),
+            pltpu.VMEM((table + LANES, eb), bf16),
+            pltpu.VMEM((blocks, span, eb), bf16),
             pltpu.VMEM((blocks, LANES, eb), bf16),
             pltpu.VMEM((blocks, features, eb), bf16),
             pltpu.VMEM((blocks, features, eb), bf16),
@@ -627,11 +767,10 @@
             pltpu.VMEM((blocks, 16, eb), f32),
             pltpu.VMEM((blocks, features, eb), bf16),
             pltpu.VMEM((blocks, 64, eb), f32),
-            pltpu.VMEM((9 * chans, atoms), f32),
-            pltpu.VMEM((9 * chans, atoms), bf16),
-            pltpu.VMEM((9 * chans, atoms), f32),
+            pltpu.VMEM((atoms // span, 9 * chans, span), f32),
+            pltpu.VMEM((atoms // span, 9 * chans, span), bf16),
             pltpu.VMEM((6 * hpad, LANES), f32),
-            pltpu.VMEM((64, LANES), f32),
+            pltpu.VMEM((atoms // span, 16, span), f32),
         ],
         smem=2,
         limit=big,

time: 108 us -> 106 us (0.981)
  Pallas kernels: 70.8 us -> 61.5 us
  waiting for transfers between devices: 15 us -> 22.6 us
  local copies, waits for them, and re-layouts: 5.95 us -> 7.42 us
  starting transfers between devices: 14.1 us -> 12.7 us
    pallas_call x9 -> x10, Pallas kernels: 70.8 us -> 61.5 us  [call(): pl.pallas_call(kernel, out_shape=out_shape, in_specs=[scalar] * smem + [v...]
    ppermute x10, waiting for transfers between devices: 12 us -> 19 us  [shifted(): lax.ppermute(x, axis, [((i + step) % count, i) for i in range(count)])]
    unnamed x50, local copies, waits for them, and re-layouts: 5.95 us -> 7.42 us
  transfers between devices with their start and end apart: 12 -> 12, of which waited for: 7 -> 6; matrix products, arithmetic and copies ran while one was open for 0% -> 0% of each run, Pallas kernels for 6% -> 8%
where the time goes in v3:
time: 106 us
  Pallas kernels  61.5 us (58%)
  waiting for transfers between devices  22.6 us (21%)
  starting transfers between devices  12.7 us (12%)
  local copies, waits for them, and re-layouts  7.42 us (7%)
  between operations  1.52 us (1%)
    pallas_call x10, Pallas kernels, call(): pl.pallas_call(kernel, out_shape=out_shape, in_specs=[scalar] * smem + [v...  61.5 us
    ppermute x10, waiting for transfers between devices, shifted(): lax.ppermute(x, axis, [((i + step) % count, i) for i in range(count)])  19 us
    ppermute x10, starting transfers between devices, shifted(): lax.ppermute(x, axis, [((i + step) % count, i) for i in range(count)])  11.1 us
    unnamed x50, local copies, waits for them, and re-layouts  7.42 us
    ppermute x2, waiting for transfers between devices, swapped(): return lax.ppermute(x, 'gz', [(i, i ^ 1) for i in range(count)])  3.58 us
  transfers between devices with their start and end apart: 12, of which 6 were waited for; matrix products, arithmetic and copies ran while one was open for 0% of the time, Pallas kernels for 8%

profile of v3, /device:TPU:0, one launch (start us, length us, event | category | flops | bytes accessed | tf_op | source)
XLA Modules:
  0.0 105.7 jit_solution(8507014312178662077)
XLA Ops:
  0.6 2.3 %shard_map.140 = (bf16[144,512]{1,0:T(8,128)(2,1)}, bf16[144,384]{1,0:T(8,128)(2,1)}, bf16[144,384]{1,0:T(8,128)(2,1)}, bf16[144,384]{1,0:T(8,128)(2,1)}, bf16[144,384]{1,0:T(8,128)(2,1)}) custom-call(f32[3,1,512]{2,1,0:T(1,128)} %bitcast.24, bf16[512,128]{1,0:T(8,128)(2,1)} %bitcast.23, s32[8,128]{1,0:T(8,128)} %bitcast.26), custom_call_target="tpu_custom_call" | custom-call | tf_op jit(solution)/shard_map/pallas_call | solution.py:615
  2.9 3.0 %collective-permute-start = (bf16[144,384]{1,0:T(8,128)(2,1)}, bf16[144,384]{1,0:T(8,128)(2,1)S(1)}, u32[]{:S(2)}, u32[]{:S(2)}) collective-permute-start(bf16[144,384]{1,0:T(8,128)(2,1)} %get-tuple-element.49), channel_id=1, source_target_pairs={{6,0},{0,2},{2,4},{4,6},{7,1},{1,3},{3,5},{5,7},{14,8},{8,10},{10,... | collective-permute-start | bytes 331784 | tf_op jit(solution)/shard_map/ppermute | solution.py:627
  5.9 2.0 %collective-permute-start.1 = (bf16[144,384]{1,0:T(8,128)(2,1)}, bf16[144,384]{1,0:T(8,128)(2,1)S(1)}, u32[]{:S(2)}, u32[]{:S(2)}) collective-permute-start(bf16[144,384]{1,0:T(8,128)(2,1)} %get-tuple-element.50), channel_id=1, source_target_pairs={{2,0},{4,2},{6,4},{0,6},{3,1},{5,3},{7,5},{1,7},{10,8},{12,10},{14... | collective-permute-start | bytes 331784 | tf_op jit(solution)/shard_map/ppermute | solution.py:627
  8.0 1.8 %collective-permute-start.3 = (bf16[144,384]{1,0:T(8,128)(2,1)}, bf16[144,384]{1,0:T(8,128)(2,1)S(1)}, u32[]{:S(2)}, u32[]{:S(2)}) collective-permute-start(bf16[144,384]{1,0:T(8,128)(2,1)} %get-tuple-element.61), channel_id=1, source_target_pairs={{8,0},{16,8},{24,16},{0,24},{9,1},{17,9},{25,17},{1,25},{10,2},{18... | collective-permute-start | bytes 331784 | tf_op jit(solution)/shard_map/ppermute | solution.py:627
  11.1 0.7 copy-done.12
  11.9 2.0 %shard_map.141 = (s32[56,128]{1,0:T(8,128)S(1)}, s32[56,128]{1,0:T(8,128)S(1)}, s32[2,128]{1,0:T(2,128)S(1)}) custom-call(s32[1]{0:T(128)} %bitcast.16.count_ref, s32[48,128]{1,0:T(8,128)S(1)} %bitcast.21, s32[48,128]{1,0:T(8,128)S(1)} %bitcast.22), custom_call_target="tpu_custom_call" | custom-call | tf_op jit(solution)/shard_map/pallas_call | solution.py:615
  14.6 1.6 %shard_map.142 = (bf16[144,256]{1,0:T(8,128)(2,1)}, bf16[144,256]{1,0:T(8,128)(2,1)}) custom-call(bf16[144,384]{1,0:T(8,128)(2,1)} %copy-done.14, bf16[144,384]{1,0:T(8,128)(2,1)} %copy-done.15), custom_call_target="tpu_custom_call" | custom-call | tf_op jit(solution)/shard_map/pallas_call | solution.py:615
  16.3 1.7 %collective-permute-start.5 = (bf16[144,256]{1,0:T(8,128)(2,1)}, bf16[144,256]{1,0:T(8,128)(2,1)S(1)}, u32[]{:S(2)}, u32[]{:S(2)}) collective-permute-start(bf16[144,256]{1,0:T(8,128)(2,1)} %get-tuple-element.63), channel_id=1, source_target_pairs={{8,0},{16,8},{24,16},{0,24},{9,1},{17,9},{25,17},{1,25},{10,2},{18... | collective-permute-start | bytes 221192 | tf_op jit(solution)/shard_map/ppermute | solution.py:627
  18.0 2.2 %shard_map.143 = (bf16[256,128]{1,0:T(8,128)(2,1)}, bf16[256,128]{1,0:T(8,128)(2,1)}, bf16[256,64]{1,0:T(8,128)(2,1)}, bf16[256,256]{1,0:T(8,128)(2,1)}, bf16[25...) custom-call(bf16[128,256]{1,0:T(8,128)(2,1)} %w_emb_ref.1, ...), custom_call_target="tpu_custom_call" | custom-call | tf_op jit(solution)/shard_map/pallas_call | solution.py:615
  21.0 2.3 %shard_map.144 = (bf16[144,2560]{1,0:T(8,128)(2,1)}, bf16[144,128]{1,0:T(8,128)(2,1)}) custom-call(f32[3,1,512]{2,1,0:T(1,128)} %bitcast.25, bf16[144,512]{1,0:T(8,128)(2,1)} %get-tuple-element.57.own_ref, s32[1,128]{1,0:T(1,128)} %bitcast.29, bf16[144,384]{1,0:T(8,128)(2,1)} %copy-done.14, bf16[144,384]{1,0:T(8,128)(2,1)} %copy-done.15, ...), custom_call_target="tpu_custom_call" | custom-call | tf_op jit(solution)/shard_map/pallas_call | solution.py:615
  23.4 1.6 %collective-permute-start.6 = (bf16[144,128]{1,0:T(8,128)(2,1)}, bf16[144,128]{1,0:T(8,128)(2,1)S(1)}, u32[]{:S(2)}, u32[]{:S(2)}) collective-permute-start(bf16[144,128]{1,0:T(8,128)(2,1)} %get-tuple-element.78), channel_id=1, source_target_pairs={{0,1},{1,0},{2,3},{3,2},{4,5},{5,4},{6,7},{7,6},{8,9},{9,8},{10,11... | collective-permute-start | bytes 110600 | tf_op jit(solution)/shard_map/ppermute | solution.py:632
  25.0 2.9 %shard_map.145 = (bf16[256,2560]{1,0:T(8,128)(2,1)}, f32[6,24,128]{2,1,0:T(8,128)}) custom-call(bf16[144,2560]{1,0:T(8,128)(2,1)} %get-tuple-element.74.inner_ref, bf16[256,128]{1,0:T(8,128)(2,1)} %get-tuple-element.75.w_emb_ref), custom_call_target="tpu_custom_call" | custom-call | tf_op jit(solution)/shard_map/pallas_call | solution.py:615
  28.0 1.3 %copy-done = bf16[256,2560]{1,0:T(8,128)(2,1)S(1)} copy-done((bf16[256,2560]{1,0:T(8,128)(2,1)S(1)}, bf16[256,2560]{1,0:T(8,128)(2,1)}, u32[]{:S(2)}) %copy-start) | copy-done | bytes 1310744
  29.3 0.9 copy-done.7
  30.2 43.5 %shard_map.146 = (f32[3,24,128]{2,1,0:T(8,128)S(1)}, f32[3,128]{1,0:T(4,128)S(1)}, f32[1,512]{1,0:T(1,128)}) custom-call(s32[2,128]{1,0:T(2,128)S(1)} %get-tuple-element.54.meta_ref, f32[1]{0:T(128)} %bitcast.6.lift_ref, s32[28,1,256]{2,1,0:T(1,128)S(1)} %bitcast.19, s32[28,1,256]{2,1,0:T(1,128)S(1)} %bitcast.20, bf16[256,2560]{1,0:T(8,128)(2,1)S(1)} %copy-done, ...), custom_call_target="tpu_custom_call" | custom-call | tf_op jit(solution)/shard_map/pallas_call | solution.py:615
  74.3 3.6 %collective-permute-done.7.back_ref = f32[3,128]{1,0:T(4,128)S(1)} collective-permute-done((f32[3,128]{1,0:T(4,128)S(1)}, f32[3,128]{1,0:T(4,128)S(1)}, u32[]{:S(2)}, u32[]{:S(2)}) %collective-permute-start.7) | collective-permute-done | bytes 1568 | tf_op jit(solution)/shard_map/ppermute | solution.py:632
  78.5 1.6 %shard_map.147 = (f32[3,8,128]{2,1,0:T(8,128)}, f32[15,128]{1,0:T(8,128)}, f32[15,128]{1,0:T(8,128)}, f32[9,128]{1,0:T(8,128)}, f32[9,128]{1,0:T(8,128)}) custom-call(f32[3,24,128]{2,1,0:T(8,128)} %copy-done.10, f32[3,128]{1,0:T(4,128)} %copy-done.24, s32[1,128]{1,0:T(1,128)} %bitcast.30), custom_call_target="tpu_custom_call" | custom-call | tf_op jit(solution)/shard_map/pallas_call | solution.py:615
  80.6 1.1 %collective-permute-done.8.from_xp_ref = f32[15,128]{1,0:T(8,128)S(1)} collective-permute-done((f32[15,128]{1,0:T(8,128)}, f32[15,128]{1,0:T(8,128)S(1)}, u32[]{:S(2)}, u32[]{:S(2)}) %collective-permute-start.8) | collective-permute-done | bytes 7712 | tf_op jit(solution)/shard_map/ppermute | solution.py:627
  81.7 14.2 %collective-permute-done.9.from_xm_ref = f32[15,128]{1,0:T(8,128)S(1)} collective-permute-done((f32[15,128]{1,0:T(8,128)}, f32[15,128]{1,0:T(8,128)S(1)}, u32[]{:S(2)}, u32[]{:S(2)}) %collective-permute-start.9) | collective-permute-done | bytes 7712 | tf_op jit(solution)/shard_map/ppermute | solution.py:627
  96.5 1.4 %shard_map.148 = (f32[9,128]{1,0:T(8,128)}, f32[9,128]{1,0:T(8,128)}) custom-call(f32[15,128]{1,0:T(8,128)} %copy-done.20, f32[15,128]{1,0:T(8,128)} %copy-done.21, f32[9,128]{1,0:T(8,128)} %get-tuple-element.92.to_ym_ref, f32[9,128]{1,0:T(8,128)} %get-tuple-element.93.to_yp_ref), custom_call_target="tpu_custom_call" | custom-call | tf_op jit(solution)/shard_map/pallas_call | solution.py:615
  97.8 2.0 %collective-permute-start.11 = (f32[9,128]{1,0:T(8,128)}, f32[9,128]{1,0:T(8,128)S(1)}, u32[]{:S(2)}, u32[]{:S(2)}) collective-permute-start(f32[9,128]{1,0:T(8,128)} %get-tuple-element.95), channel_id=1, source_target_pairs={{6,0},{0,2},{2,4},{4,6},{7,1},{1,3},{3,5},{5,7},{14,8},{8,10},{10,... | collective-permute-start | bytes 13832 | tf_op jit(solution)/shard_map/ppermute | solution.py:627
  99.8 1.8 %collective-permute-done.10.from_yp_ref = f32[9,128]{1,0:T(8,128)S(1)} collective-permute-done((f32[9,128]{1,0:T(8,128)}, f32[9,128]{1,0:T(8,128)S(1)}, u32[]{:S(2)}, u32[]{:S(2)}) %collective-permute-start.10) | collective-permute-done | bytes 4640 | tf_op jit(solution)/shard_map/ppermute | solution.py:627
  101.7 1.8 %collective-permute-done.11.from_ym_ref = f32[9,128]{1,0:T(8,128)S(1)} collective-permute-done((f32[9,128]{1,0:T(8,128)}, f32[9,128]{1,0:T(8,128)S(1)}, u32[]{:S(2)}, u32[]{:S(2)}) %collective-permute-start.11) | collective-permute-done | bytes 4640 | tf_op jit(solution)/shard_map/ppermute | solution.py:627
  104.1 1.7 %shard_map.149 = f32[3,1,512]{2,1,0:T(1,128)} custom-call(f32[3,8,128]{2,1,0:T(8,128)} %get-tuple-element.89.own_ref, s32[8,128]{1,0:T(8,128)} %bitcast.27, f32[15,128]{1,0:T(8,128)} %copy-done.20, f32[15,128]{1,0:T(8,128)} %copy-done.21, f32[9,128]{1,0:T(8,128)} %copy-done.22, f32[9,128]{1,0:T(8,128)} %copy-done.23), custom_call_target="tpu_custom_call" | custom-call | tf_op jit(solution)/shard_map/pallas_call | solution.py:615
  (60 shorter events, 5.2 us)
Async XLA Ops:
  0.6 27.3 %copy-start.3 = (bf16[256,64]{0,1:T(8,128)(2,1)S(1)}, bf16[256,64]{0,1:T(8,128)(2,1)}, u32[]{:S(2)}) copy-start(bf16[256,64]{0,1:T(8,128)(2,1)} %param.22) | copy-start | bytes 98308
  2.9 11.0 %collective-permute-start = (bf16[144,384]{1,0:T(8,128)(2,1)}, bf16[144,384]{1,0:T(8,128)(2,1)S(1)}, u32[]{:S(2)}, u32[]{:S(2)}) collective-permute-start(bf16[144,384]{1,0:T(8,128)(2,1)} %get-tuple-element.49), channel_id=1, source_target_pairs={{6,0},{0,2},{2,4},{4,6},{7,1},{1,3},{3,5},{5,7},{14,8},{8,10},{10,... | collective-permute-start | bytes 331784 | tf_op jit(solution)/shard_map/ppermute | solution.py:627
  5.9 8.0 %collective-permute-start.1 = (bf16[144,384]{1,0:T(8,128)(2,1)}, bf16[144,384]{1,0:T(8,128)(2,1)S(1)}, u32[]{:S(2)}, u32[]{:S(2)}) collective-permute-start(bf16[144,384]{1,0:T(8,128)(2,1)} %get-tuple-element.50), channel_id=1, source_target_pairs={{2,0},{4,2},{6,4},{0,6},{3,1},{5,3},{7,5},{1,7},{10,8},{12,10},{14... | collective-permute-start | bytes 331784 | tf_op jit(solution)/shard_map/ppermute | solution.py:627
  8.0 12.4 %collective-permute-start.2 = (bf16[144,384]{1,0:T(8,128)(2,1)}, bf16[144,384]{1,0:T(8,128)(2,1)S(1)}, u32[]{:S(2)}, u32[]{:S(2)}) collective-permute-start(bf16[144,384]{1,0:T(8,128)(2,1)} %get-tuple-element.60), channel_id=1, source_target_pairs={{24,0},{0,8},{8,16},{16,24},{25,1},{1,9},{9,17},{17,25},{26,2},{2,... | collective-permute-start | bytes 331784 | tf_op jit(solution)/shard_map/ppermute | solution.py:627
  8.0 12.4 %collective-permute-start.3 = (bf16[144,384]{1,0:T(8,128)(2,1)}, bf16[144,384]{1,0:T(8,128)(2,1)S(1)}, u32[]{:S(2)}, u32[]{:S(2)}) collective-permute-start(bf16[144,384]{1,0:T(8,128)(2,1)} %get-tuple-element.61), channel_id=1, source_target_pairs={{8,0},{16,8},{24,16},{0,24},{9,1},{17,9},{25,17},{1,25},{10,2},{18... | collective-permute-start | bytes 331784 | tf_op jit(solution)/shard_map/ppermute | solution.py:627
  16.2 4.0 %collective-permute-start.4 = (bf16[144,256]{1,0:T(8,128)(2,1)}, bf16[144,256]{1,0:T(8,128)(2,1)S(1)}, u32[]{:S(2)}, u32[]{:S(2)}) collective-permute-start(bf16[144,256]{1,0:T(8,128)(2,1)} %get-tuple-element.62), channel_id=1, source_target_pairs={{24,0},{0,8},{8,16},{16,24},{25,1},{1,9},{9,17},{17,25},{26,2},{2,... | collective-permute-start | bytes 221192 | tf_op jit(solution)/shard_map/ppermute | solution.py:627
  16.3 4.0 %collective-permute-start.5 = (bf16[144,256]{1,0:T(8,128)(2,1)}, bf16[144,256]{1,0:T(8,128)(2,1)S(1)}, u32[]{:S(2)}, u32[]{:S(2)}) collective-permute-start(bf16[144,256]{1,0:T(8,128)(2,1)} %get-tuple-element.63), channel_id=1, source_target_pairs={{8,0},{16,8},{24,16},{0,24},{9,1},{17,9},{25,17},{1,25},{10,2},{18... | collective-permute-start | bytes 221192 | tf_op jit(solution)/shard_map/ppermute | solution.py:627
  20.2 7.7 %copy-start.1 = (bf16[256,128]{1,0:T(8,128)(2,1)S(1)}, bf16[256,128]{1,0:T(8,128)(2,1)}, u32[]{:S(2)}) copy-start(bf16[256,128]{1,0:T(8,128)(2,1)} %get-tuple-element.75.w_emb_ref) | copy-start | bytes 196612
  20.2 7.7 %copy-start.2 = (bf16[448,256]{1,0:T(8,128)(2,1)S(1)}, bf16[448,256]{1,0:T(8,128)(2,1)}, u32[]{:S(2)}) copy-start(bf16[448,256]{1,0:T(8,128)(2,1)} %get-tuple-element.83.w_back_ref) | copy-start | bytes 688132
  20.2 7.7 %copy-start.4 = (bf16[256,256]{1,0:T(8,128)(2,1)S(1)}, bf16[256,256]{1,0:T(8,128)(2,1)}, u32[]{:S(2)}) copy-start(bf16[256,256]{1,0:T(8,128)(2,1)} %get-tuple-element.81.w_lat_t_ref) | copy-start | bytes 393220
  20.2 7.7 %copy-start.5 = (bf16[256,192]{1,0:T(8,128)(2,1)S(1)}, bf16[256,192]{1,0:T(8,128)(2,1)}, u32[]{:S(2)}) copy-start(bf16[256,192]{1,0:T(8,128)(2,1)} %get-tuple-element.82.w_ten_t_ref) | copy-start | bytes 294916
  20.2 7.7 %copy-start.6 = (f32[256,128]{1,0:T(8,128)S(1)}, f32[256,128]{1,0:T(8,128)}, u32[]{:S(2)}) copy-start(f32[256,128]{1,0:T(8,128)} %get-tuple-element.84.w_out_ref) | copy-start | bytes 393220
  20.2 7.7 %copy-start.8 = (bf16[256,128]{1,0:T(8,128)(2,1)S(1)}, bf16[256,128]{1,0:T(8,128)(2,1)}, u32[]{:S(2)}) copy-start(bf16[256,128]{1,0:T(8,128)(2,1)} %get-tuple-element.79.w_rad_ref) | copy-start | bytes 196612
  20.2 7.7 %copy-start.9 = (bf16[256,64]{1,0:T(8,128)(2,1)S(1)}, bf16[256,64]{1,0:T(8,128)(2,1)}, u32[]{:S(2)}) copy-start(bf16[256,64]{1,0:T(8,128)(2,1)} %get-tuple-element.80.w_chan_ref) | copy-start | bytes 98308
  20.2 7.7 %copy-start.13 = (bf16[16,256]{1,0:T(8,128)(2,1)S(1)}, bf16[16,256]{1,0:T(8,128)(2,1)}, u32[]{:S(2)}) copy-start(bf16[16,256]{1,0:T(8,128)(2,1)} %get-tuple-element.85.w_rbf_ref) | copy-start | bytes 24580
  23.4 4.5 %collective-permute-start.6 = (bf16[144,128]{1,0:T(8,128)(2,1)}, bf16[144,128]{1,0:T(8,128)(2,1)S(1)}, u32[]{:S(2)}, u32[]{:S(2)}) collective-permute-start(bf16[144,128]{1,0:T(8,128)(2,1)} %get-tuple-element.78), channel_id=1, source_target_pairs={{0,1},{1,0},{2,3},{3,2},{4,5},{5,4},{6,7},{7,6},{8,9},{9,8},{10,11... | collective-permute-start | bytes 110600 | tf_op jit(solution)/shard_map/ppermute | solution.py:632
  28.0 1.3 %copy-start = (bf16[256,2560]{1,0:T(8,128)(2,1)S(1)}, bf16[256,2560]{1,0:T(8,128)(2,1)}, u32[]{:S(2)}) copy-start(bf16[256,2560]{1,0:T(8,128)(2,1)} %get-tuple-element.76.feat_in_ref) | copy-start | bytes 3932164
  74.3 3.6 %collective-permute-start.7 = (f32[3,128]{1,0:T(4,128)S(1)}, f32[3,128]{1,0:T(4,128)S(1)}, u32[]{:S(2)}, u32[]{:S(2)}) collective-permute-start(f32[3,128]{1,0:T(4,128)S(1)} %get-tuple-element.88), channel_id=1, source_target_pairs={{0,1},{1,0},{2,3},{3,2},{4,5},{5,4},{6,7},{7,6},{8,9},{9,8},{10,11... | collective-permute-start | bytes 4616 | tf_op jit(solution)/shard_map/ppermute | solution.py:632
  80.1 1.6 %collective-permute-start.8 = (f32[15,128]{1,0:T(8,128)}, f32[15,128]{1,0:T(8,128)S(1)}, u32[]{:S(2)}, u32[]{:S(2)}) collective-permute-start(f32[15,128]{1,0:T(8,128)} %get-tuple-element.90), channel_id=1, source_target_pairs={{8,0},{16,8},{24,16},{0,24},{9,1},{17,9},{25,17},{1,25},{10,2},{18... | collective-permute-start | bytes 23048 | tf_op jit(solution)/shard_map/ppermute | solution.py:627
  80.1 15.8 %collective-permute-start.9 = (f32[15,128]{1,0:T(8,128)}, f32[15,128]{1,0:T(8,128)S(1)}, u32[]{:S(2)}, u32[]{:S(2)}) collective-permute-start(f32[15,128]{1,0:T(8,128)} %get-tuple-element.91), channel_id=1, source_target_pairs={{24,0},{0,8},{8,16},{16,24},{25,1},{1,9},{9,17},{17,25},{26,2},{2,... | collective-permute-start | bytes 23048 | tf_op jit(solution)/shard_map/ppermute | solution.py:627
  81.7 14.2 %copy-start.20 = (f32[15,128]{1,0:T(8,128)}, f32[15,128]{1,0:T(8,128)S(1)}, u32[]{:S(2)}) copy-start(f32[15,128]{1,0:T(8,128)S(1)} %collective-permute-done.8.from_xp_ref) | copy-start | bytes 23044
  97.8 3.9 %collective-permute-start.10 = (f32[9,128]{1,0:T(8,128)}, f32[9,128]{1,0:T(8,128)S(1)}, u32[]{:S(2)}, u32[]{:S(2)}) collective-permute-start(f32[9,128]{1,0:T(8,128)} %get-tuple-element.94), channel_id=1, source_target_pairs={{2,0},{4,2},{6,4},{0,6},{3,1},{5,3},{7,5},{1,7},{10,8},{12,10},{14... | collective-permute-start | bytes 13832 | tf_op jit(solution)/shard_map/ppermute | solution.py:627
  97.8 5.7 %collective-permute-start.11 = (f32[9,128]{1,0:T(8,128)}, f32[9,128]{1,0:T(8,128)S(1)}, u32[]{:S(2)}, u32[]{:S(2)}) collective-permute-start(f32[9,128]{1,0:T(8,128)} %get-tuple-element.95), channel_id=1, source_target_pairs={{6,0},{0,2},{2,4},{4,6},{7,1},{1,3},{3,5},{5,7},{14,8},{8,10},{10,... | collective-permute-start | bytes 13832 | tf_op jit(solution)/shard_map/ppermute | solution.py:627
  101.7 1.8 %copy-start.22 = (f32[9,128]{1,0:T(8,128)}, f32[9,128]{1,0:T(8,128)S(1)}, u32[]{:S(2)}) copy-start(f32[9,128]{1,0:T(8,128)S(1)} %collective-permute-done.10.from_yp_ref) | copy-start | bytes 13828
  (13 other events, 8.7 us)
